TPU v7x, 512 devices: a whole 4x4x16 slice. The times are simulated.
512 devices in a mesh: section: 4 (over y), lane: 16 (over z), group: 8 (over x, core).
Axes of the slice: x: 4, y: 4, z: 16, core: 2. Of those that a mesh axis runs over, the one named last changes fastest.
Arguments:
- raw: bfloat16 [65536, 3072], P(('section', 'lane'), 'group'), may hold values from -6 to 6
- taps: float32 [64], replicated, may hold values from -0.75 to 0.75
- whitening: bfloat16 [3072, 384], P('group'), may hold values from -0.3125 to 0.3125
- basis: bfloat16 [121, 6], replicated, may hold values from -0.5 to 0.5
- project: bfloat16 [2304, 384], replicated, may hold values from -0.125 to 0.125
- centroids: bfloat16 [8, 1024, 384], P('group'), may hold values from -40 to 40
- prior: float32 [8, 1024], P('group', 'lane'), may hold values from 0.25 to 4
- times: int32 [64, 8, 128], P(('section', 'lane'), 'group'), may hold values from 0 to 1023, as said below
- counts: int32 [64, 8], P(('section', 'lane'), 'group'), may hold values from 64 to 128
Outputs:
- snapshots: float32 [4, 8, 1024, 384], P('section', 'group', 'lane')
Inputs may be any that keep to these rules, and one draw needn't show every extreme that they name: Within each segment and probe the times do not fall.
All inputs are finite; a program needn't handle non-finite values.
Results may differ from a plain program's by a relative error of at most 0.0085.
Values may be sent and summed in bfloat16 or wider, within the bound.
No kernel may reach another device: no remote copies, remote signals or barrier semaphores. Data moves between devices by JAX's collectives and lax.ppermute only.
A program may use at most 64 MiB of HBM per device.

v0:
```python
import jax
import jax.numpy as jnp
from jax import lax
from jax.sharding import PartitionSpec as P

sharpness = 0.25


def passed_along(value, axis, steps):
    count = lax.axis_size(axis)
    first, last = (max(0, -steps), min(count, count - steps))
    return lax.ppermute(value, axis, [(source, source + steps) for source in range(first, last)])


def with_halo(block, sides, width):
    for axis, dim in sides:
        count = lax.axis_size(axis)
        forward = [(i, i + 1) for i in range(count - 1)]
        backward = [(target, source) for source, target in forward]
        low = lax.ppermute(
            lax.slice_in_dim(block, block.shape[dim] - width, None, axis=dim), axis, forward
        )
        high = lax.ppermute(lax.slice_in_dim(block, 0, width, axis=dim), axis, backward)
        block = jnp.concatenate([low, block, high], axis=dim)
    return block


def prefix(value, axis, join, neutral):
    count, mine = (lax.axis_size(axis), lax.axis_index(axis))
    pieces = jax.tree.map(lambda part: lax.all_gather(part, axis), value)
    subtotal = jax.tree.map(
        lambda part, zero: jnp.full_like(part, 0) + jnp.asarray(zero, part.dtype), value, neutral
    )

    def turn(position, subtotal):
        longer = join(subtotal, jax.tree.map(lambda part: part[position], pieces))
        return jax.tree.map(lambda new, old: jnp.where(position < mine, new, old), longer, subtotal)

    return lax.fori_loop(0, count - 1, turn, subtotal)


def run_filter(extended, taps, out_rows):
    num_taps = taps.shape[0]
    total = jnp.zeros((out_rows, extended.shape[1]), jnp.float32)
    for tap_index in range(num_taps):
        start = num_taps - 1 - tap_index
        total = total + taps[tap_index] * extended[start : start + out_rows].astype(jnp.float32)
    return total


def add_pairs(earlier, later):
    return (earlier[0] + later[0], earlier[1] + later[1])


def all_components(padded, basis, seg_len):
    snip_len = basis.shape[0]
    ranks = basis.shape[1]
    channels = padded.shape[1]
    block_rows = 128
    window = block_rows + snip_len - 1
    offset = (
        jnp.arange(window, dtype=jnp.int32)[None, :]
        - jnp.arange(block_rows, dtype=jnp.int32)[:, None]
    )
    picker = (offset[:, :, None] == jnp.arange(snip_len, dtype=jnp.int32)[None, None, :]).astype(
        jnp.bfloat16
    )
    band = jnp.einsum("tjv,vr->trj", picker, basis, preferred_element_type=jnp.float32).astype(
        jnp.bfloat16
    )
    band = band.reshape(block_rows * ranks, window)
    block_starts = jnp.arange(seg_len // block_rows, dtype=jnp.int32) * block_rows

    def one_block(begin):
        rows = lax.dynamic_slice_in_dim(padded, begin, window, 0)
        return jnp.dot(band, rows, preferred_element_type=jnp.float32).astype(jnp.bfloat16)

    comps = jax.vmap(one_block)(block_starts)
    return comps.reshape(seg_len, ranks * channels)


def per_device(raw, taps, whitening, basis, project, centroids, prior, times, counts):
    seg_len = raw.shape[0]
    num_taps = taps.shape[0]
    half_span = (basis.shape[0] - 1) // 2
    before = passed_along(raw[seg_len - (num_taps - 1) :], ("section", "lane"), 1)
    extended = jnp.concatenate([before, raw], axis=0)
    trace = run_filter(extended, taps, seg_len).astype(jnp.bfloat16)
    white = jnp.dot(trace, whitening, preferred_element_type=jnp.float32).astype(jnp.bfloat16)
    padded = with_halo(white, ((("section", "lane"), 0),), half_span)
    spike_slots = times.shape[2]
    comps_all = all_components(padded, basis, seg_len)
    chooser = (times[0, 0][:, None] == jnp.arange(seg_len, dtype=jnp.int32)[None, :]).astype(
        jnp.bfloat16
    )
    comps = jnp.dot(chooser, comps_all, preferred_element_type=jnp.float32).astype(jnp.bfloat16)
    feats = jnp.dot(comps, project, preferred_element_type=jnp.float32).astype(jnp.bfloat16)
    live_rows = (jnp.arange(spike_slots, dtype=jnp.int32) < counts[0, 0]).astype(jnp.bfloat16)
    spikes, live_all = (
        lax.all_gather(feats, "group", axis=0, tiled=True),
        lax.all_gather(live_rows, "group", axis=0, tiled=True),
    )
    centers = centroids[0]
    logits = (
        lax.dot_general(
            spikes, centers, (((1,), (1,)), ((), ())), preferred_element_type=jnp.float32
        )
        * sharpness
    )
    local_top = jnp.max(logits, axis=1)
    top = lax.pmax(local_top, "group")
    local_total = jnp.sum(jnp.exp(logits - top[:, None]), axis=1)
    total = lax.psum(local_total, "group")
    lse = top + jnp.log(total)
    resp = (jnp.exp(logits - lse[:, None]) * live_all.astype(jnp.float32)[:, None]).astype(
        jnp.bfloat16
    )
    sums = lax.dot_general(
        resp, spikes, (((0,), (0,)), ((), ())), preferred_element_type=jnp.float32
    )
    mass = jnp.sum(resp, axis=0, dtype=jnp.float32)
    own_sums, own_mass = (
        lax.psum_scatter(sums, "lane", scatter_dimension=0, tiled=True),
        lax.psum_scatter(mass, "lane", scatter_dimension=0, tiled=True),
    )
    earlier_sums, earlier_mass = prefix(
        (own_sums, own_mass),
        "section",
        add_pairs,
        (jnp.zeros_like(own_sums), jnp.zeros_like(own_mass)),
    )
    run_sums = earlier_sums + own_sums
    run_mass = earlier_mass + own_mass
    cent_rows = own_sums.shape[0]
    start_centers = lax.dynamic_slice_in_dim(
        centers, lax.axis_index("lane") * cent_rows, cent_rows, 0
    ).astype(jnp.float32)
    weights = prior[0]
    numer = weights[:, None] * start_centers + run_sums
    snap = numer / (weights + run_mass)[:, None]
    return snap[None, None]


def solution(mesh):
    placed = (
        P(("section", "lane"), "group"),
        P(),
        P("group", None),
        P(),
        P(),
        P("group", None, None),
        P("group", "lane"),
        P(("section", "lane"), "group", None),
        P(("section", "lane"), "group"),
    )
    return jax.shard_map(
        per_device,
        mesh=mesh,
        in_specs=placed,
        out_specs=P("section", "group", "lane", None),
        check_vma=False,
    )
```

profile of v0, /device:TPU:4, one launch (start us, length us, event | category | flops | bytes accessed | tf_op | source)
XLA Modules:
  0.0 284.1 jit_solution(1336686541782878980)
XLA Ops:
  6.5 0.9 slice.392
  7.5 3.8 %collective-permute-start = (bf16[63,384]{1,0:T(8,128)(2,1)S(1)}, bf16[63,384]{1,0:T(8,128)(2,1)S(1)}, u32[]{:S(2)}, u32[]{:S(2)}) collective-permute-start(bf16[63,384]{1,0:T(8,128)(2,1)S(1)} %slice.392), channel_id=1, source_target_pairs={{0,8},{8,16},{16,24},{24,32},{32,40},{40,48},{48,56},{56,64},{64,7... | collective-permute-start | bytes 145160 | tf_op jit(solution)/shard_map/ppermute | solution.py:12
  11.3 2.1 fusion.84
  13.4 2.1 fusion.83
  15.5 2.1 fusion.82
  17.6 1.6 fusion.85
  19.2 6.5 %fusion.3 = bf16[128,6,248]{0,1,2:T(8,128)(2,1)S(1)} fusion(s32[128,248]{0,1:T(8,128)S(1)} %iota_subtract_fusion, bf16[121,6]{0,1:T(8,128)(2,1)} %param.14), kind=kOutput, calls=%fused_computation.79 | convolution fusion | flops 50123776 | bytes 509356 | tf_op jit(solution)/shard_map/tjv,vr->trj/dot_general | solution.py:68
  26.4 56.1 %convolution_convert_fusion.1 = bf16[1024,384]{1,0:T(8,128)(2,1)S(1)} fusion(bf16[384,384]{1,0:T(8,128)(2,1)S(1)} %copy-done.7, bf16[1024,384]{1,0:T(8,128)(2,1)S(1)} %copy-done.4, bf16[63,384]{1,0:T(8,128)(2,1)S(1)} %collective-permute-done, f32[]{:T(128)} %bitcast.69, f32[]{:T(128)} %bitcast.68, f32[]{:T(128)} %bitcast.67, f32[]{:T(128)} %bitcast.66, ...), kind=kOutput, calls=%fused_computation.77 | convolution fusion | flops 452198400 | bytes 1916416 | tf_op jit(solution)/shard_map/dot_general | solution.py:89
  82.4 0.9 copy-done.1
  83.3 3.8 %collective-permute-start.1 = (bf16[60,384]{1,0:T(8,128)(2,1)S(1)}, bf16[60,384]{1,0:T(8,128)(2,1)S(1)}, u32[]{:S(2)}, u32[]{:S(2)}) collective-permute-start(bf16[60,384]{1,0:T(8,128)(2,1)S(1)} %get-tuple-element.167), channel_id=1, source_target_pairs={{0,8},{8,16},{16,24},{24,32},{32,40},{40,48},{48,56},{56,64},{64,7... | collective-permute-start | bytes 138248 | tf_op jit(solution)/shard_map/ppermute | solution.py:20
  87.2 1.3 collective-permute-start.2
  88.5 0.6 copy.12
  89.3 8.5 %all-gather.2 = bf16[8,1,128]{2,1,0:T(2,128)(2,1)S(1)} all-gather(bf16[1,1,128]{2,1,0:T(2,128)(2,1)S(1)} %fusion.78), channel_id=1, replica_groups=mesh['section'=4,'lane'=16,'group'=8] {'group'}, dimensions={0}, use_global_device_ids=true | all-gather | bytes 2304 | tf_op jit(solution)/shard_map/all_gather | solution.py:101
  97.8 4.2 %concatenate.10 = bf16[1144,384]{1,0:T(8,128)(2,1)S(1)} concatenate(bf16[60,384]{1,0:T(8,128)(2,1)S(1)} %collective-permute-done.1, bf16[1024,384]{1,0:T(8,128)(2,1)} %copy-done.1, bf16[60,384]{1,0:T(8,128)(2,1)S(1)} %collective-permute-done.2), dimensions={0} | concatenate | bytes 1757184 | tf_op jit(solution)/shard_map/concatenate | solution.py:24
  102.1 16.8 %while.17 = (s32[]{:T(128)}, bf16[1144,384]{1,0:T(8,128)(2,1)S(1)}, s32[8,2]{0,1:T(2,128)S(1)}, bf16[8,248,384]{2,1,0:T(8,128)(2,1)}, s32[]{:T(128)}) while((s32[]{:T(128)}, bf16[1144,384]{1,0:T(8,128)(2,1)S(1)}, s32[8,2]{0,1:T(2,128)S(1)}, bf16[8,248,384]{2,1,0:T(8,128)(2,1)}, s32[]{:T(128)}) %tuple.105), condition=%wide.while_cond, body=%wide.while_body.sunk | while | flops 2 | bytes 382041 | solution.py:75
  102.2 0.6 slice.1230
  102.8 1.4 bitcast_dynamic-update-slice_fusion.2
  104.2 0.6 slice.1230
  104.8 1.4 bitcast_dynamic-update-slice_fusion.2
  106.3 0.6 slice.1230
  106.9 1.4 bitcast_dynamic-update-slice_fusion.2
  108.4 0.6 slice.1230
  109.0 1.4 bitcast_dynamic-update-slice_fusion.2
  110.5 0.6 slice.1230
  111.1 1.4 bitcast_dynamic-update-slice_fusion.2
  112.6 0.6 slice.1230
  113.2 1.4 bitcast_dynamic-update-slice_fusion.2
  114.7 0.6 slice.1230
  115.3 1.4 bitcast_dynamic-update-slice_fusion.2
  116.8 0.6 slice.1230
  117.4 1.4 bitcast_dynamic-update-slice_fusion.2
  118.8 4.9 %convert_bitcast_fusion = bf16[8,768,384]{2,1,0:T(8,128)(2,1)} fusion(bf16[8,248,384]{2,1,0:T(8,128)(2,1)} %get-tuple-element.124, bf16[768,248]{1,0:T(8,128)(2,1)S(1)} %reshape.43), kind=kOutput, calls=%fused_computation.70 | convolution fusion | flops 1172570112 | bytes 6623232 | tf_op jit(solution)/shard_map/vmap()/dot_general | solution.py:76
  123.7 9.1 %reshape.44 = bf16[1024,2304]{1,0:T(8,128)(2,1)} reshape(bf16[8,768,384]{2,1,0:T(8,128)(2,1)} %convert_bitcast_fusion) | data formatting | bytes 9437184 | tf_op jit(solution)/shard_map/reshape | solution.py:79
  132.8 3.5 %fusion.5 = bf16[128,384]{1,0:T(8,128)(2,1)S(1)} fusion(bf16[2304,384]{1,0:T(8,128)(2,1)S(1)} %copy-done, bf16[1024,2304]{1,0:T(8,128)(2,1)} %reshape.44, s32[128]{0:T(128)S(1)} %bitcast.120), kind=kOutput, calls=%fused_computation.81 | convolution fusion | flops 830947328 | bytes 6586880 | tf_op jit(solution)/shard_map/dot_general | solution.py:97
  136.4 14.1 %all_gather.18 = bf16[1024,384]{1,0:T(8,128)(2,1)S(1)} all-gather(bf16[128,384]{1,0:T(8,128)(2,1)S(1)} %fusion.5), channel_id=1, replica_groups=mesh['section'=4,'lane'=16,'group'=8] {'group'}, dimensions={0}, use_global_device_ids=true | all-gather | bytes 884736 | tf_op jit(solution)/shard_map/all_gather | solution.py:100
  150.4 3.2 %multiply_reduce_fusion = (f32[1024]{0:T(1024)S(1)}, f32[1024,1024]{0,1:T(8,128)}) fusion(bf16[1024,384]{1,0:T(8,128)(2,1)S(1)} %all_gather.18, bf16[1,1024,384]{2,1,0:T(8,128)(2,1)S(1)} %copy-done.2), kind=kOutput, calls=%fused_computation.74 | convolution fusion | flops 807402496 | bytes 5771264 | tf_op jit(solution)/shard_map/dot_general | solution.py:105
  153.7 10.3 %pmax.7 = f32[1024]{0:T(1024)S(1)} all-reduce(f32[1024]{0:T(1024)S(1)} %get-tuple-element.232), channel_id=1, replica_groups=mesh['section'=4,'lane'=16,'group'=8] {'group'}, use_global_device_ids=true, to_apply=%region_1.0 | all-reduce | flops 1024 | bytes 8192 | tf_op jit(solution)/shard_map/pmax | solution.py:111
  164.0 2.9 %exponential_reduce_fusion = f32[1024]{0:T(1024)S(1)} fusion(f32[1024,1024]{0,1:T(8,128)} %get-tuple-element.233, f32[1024]{0:T(1024)S(1)} %pmax.7), kind=kLoop, calls=%fused_computation.73 | loop fusion | flops 3144704 | bytes 4202496 | tf_op jit(solution)/shard_map/reduce_sum | solution.py:112
  166.9 11.9 %psum.7 = f32[1024]{0:T(1024)S(1)} all-reduce(f32[1024]{0:T(1024)S(1)} %exponential_reduce_fusion), channel_id=1, replica_groups=mesh['section'=4,'lane'=16,'group'=8] {'group'}, use_global_device_ids=true, to_apply=%region_3.0 | all-reduce | flops 1024 | bytes 8192 | tf_op jit(solution)/shard_map/psum | solution.py:113
  178.8 4.6 %fusion.76 = f32[1024,384]{1,0:T(8,128)} fusion(bf16[1024,384]{1,0:T(8,128)(2,1)S(1)} %all_gather.18, f32[1024,1024]{0,1:T(8,128)} %get-tuple-element.233, f32[1024]{0:T(1024)S(1)} %bitcast.117, f32[1024]{0:T(1024)S(1)} %log_add_fusion), kind=kOutput, calls=%fused_computation.160 | convolution fusion | flops 809500672 | bytes 6561792 | tf_op jit(solution)/shard_map/dot_general | solution.py:118
  183.5 1.3 dynamic-slice.5
  185.4 1.3 dynamic-slice.6
  187.4 3.1 %convert_reduce_fusion = f32[1024]{0:T(1024)S(1)} fusion(f32[1024]{0:T(1024)S(1)} %bitcast.118, f32[1024]{0:T(1024)S(1)} %log_add_fusion, f32[1024,1024]{0,1:T(8,128)} %get-tuple-element.233), kind=kLoop, calls=%fused_computation.71 | loop fusion | flops 6290432 | bytes 4206592 | tf_op jit(solution)/shard_map/reduce_sum | solution.py:121
  190.5 35.4 %all-reduce.2 = f32[1024]{0:T(1024)S(1)} all-reduce(f32[1024]{0:T(1024)S(1)} %convert_reduce_fusion), channel_id=5, replica_groups=mesh['section'=4,'lane'=16,'group'=8] {'lane'}, use_global_device_ids=true, to_apply=%region_6.0.clone | all-reduce | flops 1024 | bytes 8192
  226.1 10.7 %all-reduce.1 = f32[256]{0:T(256)S(1)} all-reduce(f32[256]{0:T(256)S(1)} %dynamic-slice_dynamic-update-slice_fusion), channel_id=3, replica_groups=mesh['section'=4,'lane'=16,'group'=8] {'section'}, use_global_device_ids=true, to_apply=%add.1 | all-reduce | flops 256 | bytes 2048
  236.8 26.1 %reduce-scatter.2.cloned.1.call-done = f32[64,384]{1,0:T(8,128)} async-done(((f32[1024,384]{1,0:T(8,128)}), f32[64,384]{1,0:T(8,128)}) %reduce-scatter.2.cloned.1.call-update) | async-done | bytes 98320 | tf_op jit(solution)/shard_map/reduce_scatter | solution.py:123
  263.0 13.2 %all-gather = f32[256,384]{1,0:T(8,128)S(1)} all-gather(f32[64,384]{1,0:T(8,128)} %reduce-scatter.2.cloned.1.call-done), channel_id=2, replica_groups=mesh['section'=4,'lane'=16,'group'=8] {'section'}, dimensions={0}, use_global_device_ids=true | all-gather | bytes 491520 | tf_op jit(solution)/shard_map/all_gather | solution.py:30
  276.5 0.7 fusion.75
  (50 shorter events, 1.6 us)
Async XLA Ops:
  6.5 126.3 %copy-start = (bf16[2304,384]{1,0:T(8,128)(2,1)S(1)}, bf16[2304,384]{1,0:T(8,128)(2,1)}, u32[]{:S(2)}) copy-start(bf16[2304,384]{1,0:T(8,128)(2,1)} %param.15) | copy-start | bytes 5308420
  6.5 256.4 %reduce-scatter.2.cloned.1.call-start = ((), (), s32[]{:S(2)}) async-start(), calls=%async_computation.1 | async-start | bytes 1671168 | tf_op jit(solution)/shard_map/reduce_scatter | solution.py:123
  7.5 18.8 %collective-permute-start = (bf16[63,384]{1,0:T(8,128)(2,1)S(1)}, bf16[63,384]{1,0:T(8,128)(2,1)S(1)}, u32[]{:S(2)}, u32[]{:S(2)}) collective-permute-start(bf16[63,384]{1,0:T(8,128)(2,1)S(1)} %slice.392), channel_id=1, source_target_pairs={{0,8},{8,16},{16,24},{24,32},{32,40},{40,48},{48,56},{56,64},{64,7... | collective-permute-start | bytes 145160 | tf_op jit(solution)/shard_map/ppermute | solution.py:12
  19.2 7.2 %copy-start.4 = (bf16[1024,384]{1,0:T(8,128)(2,1)S(1)}, bf16[1024,384]{1,0:T(8,128)(2,1)}, u32[]{:S(2)}) copy-start(bf16[1024,384]{1,0:T(8,128)(2,1)} %param.11) | copy-start | bytes 2359300
  19.2 7.2 %copy-start.7 = (bf16[384,384]{1,0:T(8,128)(2,1)S(1)}, bf16[384,384]{1,0:T(8,128)(2,1)}, u32[]{:S(2)}) copy-start(bf16[384,384]{1,0:T(8,128)(2,1)} %param.13) | copy-start | bytes 884740
  82.4 0.9 copy-start.1
  83.3 14.5 %collective-permute-start.1 = (bf16[60,384]{1,0:T(8,128)(2,1)S(1)}, bf16[60,384]{1,0:T(8,128)(2,1)S(1)}, u32[]{:S(2)}, u32[]{:S(2)}) collective-permute-start(bf16[60,384]{1,0:T(8,128)(2,1)S(1)} %get-tuple-element.167), channel_id=1, source_target_pairs={{0,8},{8,16},{16,24},{24,32},{32,40},{40,48},{48,56},{56,64},{64,7... | collective-permute-start | bytes 138248 | tf_op jit(solution)/shard_map/ppermute | solution.py:20
  87.2 10.7 %collective-permute-start.2 = (bf16[60,384]{1,0:T(8,128)(2,1)S(1)}, bf16[60,384]{1,0:T(8,128)(2,1)S(1)}, u32[]{:S(2)}, u32[]{:S(2)}) collective-permute-start(bf16[60,384]{1,0:T(8,128)(2,1)S(1)} %get-tuple-element.166), channel_id=1, source_target_pairs={{8,0},{16,8},{24,16},{32,24},{40,32},{48,40},{56,48},{64,56},{72,6... | collective-permute-start | bytes 138248 | tf_op jit(solution)/shard_map/ppermute | solution.py:23
  123.7 9.1 %copy-start.6 = (s32[1,1,128]{2,1,0:T(1,128)S(1)}, s32[1,1,128]{2,1,0:T(1,128)}, u32[]{:S(2)}) copy-start(s32[1,1,128]{2,1,0:T(1,128)} %param.18) | copy-start | bytes 1540
  132.8 17.6 %copy-start.2 = (bf16[1,1024,384]{2,1,0:T(8,128)(2,1)S(1)}, bf16[1,1024,384]{2,1,0:T(8,128)(2,1)}, u32[]{:S(2)}) copy-start(bf16[1,1024,384]{2,1,0:T(8,128)(2,1)} %param.16) | copy-start | bytes 2359300
  190.5 85.9 %copy-start.5 = (f32[1,64]{1,0:T(1,128)S(1)}, f32[1,64]{1,0:T(1,128)}, u32[]{:S(2)}) copy-start(f32[1,64]{1,0:T(1,128)} %param.17) | copy-start | bytes 772
  263.0 13.5 %copy-start.3 = (f32[64,384]{1,0:T(8,128)S(1)}, f32[64,384]{1,0:T(8,128)}, u32[]{:S(2)}) copy-start(f32[64,384]{1,0:T(8,128)} %reduce-scatter.2.cloned.1.call-done) | copy-start | bytes 294916
Sparse Core Ops, SparseCore 0:
  183.6 79.3 reduce-scatter.1
where the time goes:
time: 286 us; the launch traced here: 284 us
  blocking collectives  104 us (36%)
  matrix products  78.9 us (28%)
  local copies, waits for them, and re-layouts  43.4 us (15%)
  waiting for transfers between devices  26.2 us (9%)
  between operations  15.6 us (5%)
  starting transfers between devices  8.94 us (3%)
  other arithmetic  6.97 us (2%)
    dot_general x1, matrix products, per_device(): jnp.dot(trace, whitening, preferred_element_type=jnp.float32)  56.1 us
    unnamed x2, blocking collectives  46.1 us
    reduce_scatter x1, waiting for transfers between devices, per_device(): lax.psum_scatter(sums, 'lane', scatter_dimension=0, tiled=True)  26.1 us
    gather x24, local copies, waits for them, and re-layouts  16.7 us
    all_gather x1, blocking collectives, per_device(): lax.all_gather(feats, 'group', axis=0, tiled=True)  14.1 us
    all_gather x1, blocking collectives, prefix(): pieces = jax.tree.map(lambda part: lax.all_gather(part, axis), value)  13.2 us
    psum x1, blocking collectives, per_device(): total = lax.psum(local_total, 'group')  11.9 us
    pmax x1, blocking collectives, per_device(): top = lax.pmax(local_top, 'group')  10.3 us
  transfers between devices with their start and end apart: 4, of which 1 were waited for; matrix products, arithmetic and copies ran while one was open for 7% of the time, Pallas kernels for 0%

commit v1 on v0

v1 whole, which is shorter than its diff:
```python
import functools
import math

import jax
import jax.numpy as jnp
from jax import lax
from jax.experimental import pallas as pl
from jax.experimental.pallas import tpu as pltpu
from jax.sharding import PartitionSpec as P

F32 = jnp.float32
BF16 = jnp.bfloat16
LOG2E = math.log2(math.e)
SHARPNESS = 0.25
DEAD = 1e30

SEG = 1024
CH = 384
FEAT = 384
SPK = 128
TAPS = 64
SNIP = 121
HALF = 60
RANKS = 6
GROUP = 8
LANES = 16
SECTIONS = 4
NEAR = 4
FAR = 4
CG = 1024
ROWS = 64
BEFORE = 128
AFTER = 64
BLOCK = 192
SPAN = BLOCK + TAPS
WHITE_ROWS = 1152
PLACE = 1280
PAY = 208
SUM_ROWS = 192
VMEM_LIMIT = 56 * 1024 * 1024

VMEM = pl.BlockSpec(memory_space=pltpu.VMEM)
SMEM = pl.BlockSpec(memory_space=pltpu.SMEM)
ANY = pl.BlockSpec(memory_space=pl.ANY)


def call(kernel, out_shape, in_specs, out_specs, scratch=(), flops=0, moved=0):
    return pl.pallas_call(
        kernel,
        out_shape=out_shape,
        in_specs=in_specs,
        out_specs=out_specs,
        scratch_shapes=list(scratch),
        compiler_params=pltpu.CompilerParams(vmem_limit_bytes=VMEM_LIMIT),
        cost_estimate=pl.CostEstimate(flops=flops, bytes_accessed=moved, transcendentals=0),
    )


def features_kernel(
    before, after, raw, taps, whitening, basis, project, times, out,
    window, band, row, snip, white, place, comps, flat, held, raw_sem, project_sem,
):
    raw_copy = pltpu.make_async_copy(raw, window.at[pl.ds(BEFORE, SEG)], raw_sem)
    raw_copy.start()
    project_copy = pltpu.make_async_copy(project, held, project_sem)
    project_copy.start()

    row[...] = jnp.zeros_like(row)
    row[0:1, 0:TAPS] = taps[...]
    spread = jnp.broadcast_to(row[0:1, :], (SPAN, SPAN))
    shifted = pltpu.roll(spread, SPAN - TAPS, 1, stride=1, stride_axis=0)
    table = jnp.transpose(shifted)[0:BLOCK, :]
    high = table.astype(BF16)
    band[0:BLOCK, :] = high
    band[BLOCK : 2 * BLOCK, :] = (table - high.astype(F32)).astype(BF16)

    snip[...] = jnp.zeros_like(snip)
    snip[0:RANKS, 0:SNIP] = basis[...].astype(F32)

    def clear(i, carry):
        place[pl.ds(pl.multiple_of(i * 32, 32), 32), :] = jnp.zeros((32, PLACE), F32)
        return carry

    lax.fori_loop(0, SPK * 8 // 32, clear, 0)
    shape = snip[...]

    def put(s, carry):
        u = times[0, 0, s] + (64 - HALF)
        start = pl.multiple_of((u >> 7) * 128, 128)
        at = pl.multiple_of(s * 8, 8)
        place[pl.ds(at, 8), pl.ds(start, 256)] = pltpu.roll(shape, u & 127, 1)
        return carry

    lax.fori_loop(0, SPK, put, 0, unroll=8)

    window[0:BEFORE, :] = before[...]
    window[BEFORE + SEG : BEFORE + SEG + AFTER, :] = after[...]
    raw_copy.wait()
    for b in range(WHITE_ROWS // BLOCK):
        rows = window[b * BLOCK : b * BLOCK + SPAN, :]
        both = jnp.dot(band[...], rows, preferred_element_type=F32)
        trace = (both[0:BLOCK] + both[BLOCK : 2 * BLOCK]).astype(BF16)
        white[b * BLOCK : (b + 1) * BLOCK, :] = jnp.dot(
            trace, whitening[...], preferred_element_type=F32
        ).astype(BF16)
    white[WHITE_ROWS:PLACE, :] = jnp.zeros((PLACE - WHITE_ROWS, CH), BF16)
    last = (lax.axis_index("section") == SECTIONS - 1) & (lax.axis_index("lane") == LANES - 1)

    @pl.when(last)
    def _():
        white[64 + SEG : WHITE_ROWS, :] = jnp.zeros((WHITE_ROWS - 64 - SEG, CH), BF16)

    for c in range(4):
        part = place[c * 256 : (c + 1) * 256, :].astype(BF16)
        found = jnp.dot(part, white[...], preferred_element_type=F32)
        for i in range(CH // 128):
            comps[i, c * 256 : (c + 1) * 256, :] = found[:, i * 128 : (i + 1) * 128]
    for r in range(RANKS):
        for i in range(CH // 128):
            flat[:, r * CH + i * 128 : r * CH + (i + 1) * 128] = comps[
                i, pl.ds(r, SPK, stride=8), :
            ].astype(BF16)
    project_copy.wait()
    out[...] = jnp.dot(flat[...], held[...], preferred_element_type=F32).astype(BF16)


def features(before, after, raw, taps, whitening, basis, project, times):
    return call(
        features_kernel,
        jax.ShapeDtypeStruct((SPK, FEAT), BF16),
        [VMEM, VMEM, ANY, VMEM, VMEM, VMEM, ANY, SMEM],
        VMEM,
        [
            pltpu.VMEM((BEFORE + SEG + AFTER, CH), BF16),
            pltpu.VMEM((2 * BLOCK, SPAN), BF16),
            pltpu.VMEM((8, SPAN), F32),
            pltpu.VMEM((8, 256), F32),
            pltpu.VMEM((PLACE, CH), BF16),
            pltpu.VMEM((SPK * 8, PLACE), F32),
            pltpu.VMEM((CH // 128, SPK * 8, 128), F32),
            pltpu.VMEM((SPK, RANKS * CH), BF16),
            pltpu.VMEM((RANKS * CH, FEAT), BF16),
            pltpu.SemaphoreType.DMA,
            pltpu.SemaphoreType.DMA,
        ],
        flops=2_500_000_000,
        moved=4_000_000,
    )(before, after, raw, taps, whitening, basis, project, times)


def scores_kernel(spikes, centers, counts, shares, weights, tops, logits):
    for b in range(4):
        block = spikes[b * 256 : (b + 1) * 256, :]
        top = None
        for k in range(4):
            part = lax.dot_general(
                centers[0, k * 256 : (k + 1) * 256, :],
                block,
                (((1,), (1,)), ((), ())),
                preferred_element_type=F32,
            ) * (SHARPNESS * LOG2E)
            logits[k * 256 : (k + 1) * 256, b * 256 : (b + 1) * 256] = part
            best = jnp.max(part, axis=0, keepdims=True)
            top = best if top is None else jnp.maximum(top, best)
        total = jnp.zeros((1, 256), F32)
        for k in range(4):
            part = jnp.exp2(logits[k * 256 : (k + 1) * 256, b * 256 : (b + 1) * 256] - top)
            total = total + jnp.sum(part, axis=0, keepdims=True)
            weights[k * 256 : (k + 1) * 256, b * 256 : (b + 1) * 256] = part.astype(BF16)
        lse = top + jnp.log2(total)
        for h in range(2):
            g = 2 * b + h
            mine = lse[:, h * 128 : (h + 1) * 128]
            slot = lax.broadcasted_iota(jnp.int32, (1, 128), 1)
            dead = (lax.axis_index("group") == g) & (slot >= counts[0, 0])
            tops[g : g + 1, :] = top[:, h * 128 : (h + 1) * 128]
            shares[:, g, :] = jnp.broadcast_to(jnp.where(dead, DEAD, mine), (GROUP, 128))


def scores(spikes, centers, counts):
    return call(
        scores_kernel,
        (
            jax.ShapeDtypeStruct((GROUP, GROUP, SPK), F32),
            jax.ShapeDtypeStruct((CG, GROUP * SPK), BF16),
            jax.ShapeDtypeStruct((GROUP, SPK), F32),
        ),
        [VMEM, VMEM, SMEM],
        (VMEM, VMEM, VMEM),
        [pltpu.VMEM((CG, GROUP * SPK), F32)],
        flops=1_000_000_000,
        moved=4_000_000,
    )(spikes, centers, counts)


def sums_kernel(shares, weights, tops, spikes, out):
    best = shares[0]
    for g in range(1, GROUP):
        best = jnp.maximum(best, shares[g])
    total = jnp.zeros_like(best)
    for g in range(GROUP):
        total = total + jnp.exp2(shares[g] - best)
    scale = jnp.exp2(tops[...] - best) / total
    ones = jnp.ones((256, 128), BF16)
    row = lax.broadcasted_iota(jnp.int32, (ROWS, 128), 0)
    lane = lax.broadcasted_iota(jnp.int32, (ROWS, 128), 1)
    pick = row == (lane & (ROWS - 1))
    front = lax.broadcasted_iota(jnp.int32, (1, 128), 1) < ROWS
    for k in range(4):
        acc = None
        for b in range(4):
            parts = []
            for h in range(2):
                g = 2 * b + h
                wide = weights[k * 256 : (k + 1) * 256, g * 128 : (g + 1) * 128].astype(F32)
                parts.append((wide * scale[g : g + 1, :]).astype(BF16))
            resp = jnp.concatenate(parts, axis=1)
            rhs = jnp.concatenate([spikes[b * 256 : (b + 1) * 256, :], ones], axis=1)
            term = jnp.dot(resp, rhs, preferred_element_type=F32)
            acc = term if acc is None else acc + term
        for i in range(4):
            owner = 4 * k + i
            far, near = owner // NEAR, owner % NEAR
            rows = acc[i * ROWS : (i + 1) * ROWS, :]
            for c in range(3):
                out[near, far, c * ROWS : (c + 1) * ROWS, :] = rows[
                    :, c * 128 : (c + 1) * 128
                ].astype(BF16)
            mass = jnp.sum(jnp.where(pick, rows[:, 384:512], 0.0), axis=0, keepdims=True)
            out[near, far, SUM_ROWS:PAY, :] = split(mass, front)


def split(mass, front):
    high = mass.astype(BF16).astype(F32)
    return jnp.broadcast_to(
        jnp.where(front, high, mass - high), (PAY - SUM_ROWS, 128)
    ).astype(BF16)


def sums(shares, weights, tops, spikes):
    return call(
        sums_kernel,
        jax.ShapeDtypeStruct((NEAR, FAR, PAY, 128), BF16),
        [VMEM] * 4,
        VMEM,
        flops=1_000_000_000,
        moved=4_000_000,
    )(shares, weights, tops, spikes)


def near_kernel(got, own, one, two, three):
    front = lax.broadcasted_iota(jnp.int32, (1, 128), 1) < ROWS
    mine = lax.axis_index("lane") // NEAR
    for d, out in enumerate((own, one, two, three)):
        far = lax.rem(mine + d, FAR)
        acc = got[0, far].astype(F32)
        for n in range(1, NEAR):
            acc = acc + got[n, far].astype(F32)
        tail = acc[SUM_ROWS : SUM_ROWS + 1, :]
        mass = tail + pltpu.roll(tail, ROWS, 1)
        out[0:SUM_ROWS, :] = acc[0:SUM_ROWS].astype(out.dtype)
        if d == 0:
            out[SUM_ROWS:PAY, :] = jnp.broadcast_to(mass, (PAY - SUM_ROWS, 128))
        else:
            out[SUM_ROWS:PAY, :] = split(mass, front)


def far_kernel(own, one, two, three, out):
    acc = one[...].astype(F32) + two[...].astype(F32) + three[...].astype(F32)
    tail = acc[SUM_ROWS:PAY, :]
    out[0:SUM_ROWS, :] = own[0:SUM_ROWS, :] + acc[0:SUM_ROWS]
    out[SUM_ROWS:PAY, :] = own[SUM_ROWS:PAY, :] + tail + pltpu.roll(tail, ROWS, 1)


def final_kernel(own, one, two, three, centers, prior, out, held, sem):
    lane_at = lax.axis_index("lane")
    copy = pltpu.make_async_copy(
        centers.at[0, pl.ds(pl.multiple_of(lane_at * ROWS, ROWS), ROWS)], held, sem
    )
    copy.start()
    acc = own[...] + one[...] + two[...] + three[...]
    row = lax.broadcasted_iota(jnp.int32, (ROWS, ROWS), 0)
    lane = lax.broadcasted_iota(jnp.int32, (ROWS, ROWS), 1)
    pick = row == lane

    def column(value):
        wide = jnp.broadcast_to(value, (ROWS, ROWS))
        return jnp.sum(jnp.where(pick, wide, 0.0), axis=1, keepdims=True)

    weight = column(prior[...])
    inverse = 1.0 / (weight + column(acc[SUM_ROWS : SUM_ROWS + 1, 0:ROWS]))
    copy.wait()
    for c in range(3):
        numer = weight * held[:, c * 128 : (c + 1) * 128].astype(F32) + acc[
            c * ROWS : (c + 1) * ROWS, :
        ]
        out[0, 0, :, c * 128 : (c + 1) * 128] = numer * inverse


def per_device(raw, taps, whitening, basis, project, centroids, prior, times, counts):
    windows = ("section", "lane")
    count = SECTIONS * LANES
    before = lax.ppermute(raw[SEG - BEFORE :], windows, [(i, i + 1) for i in range(count - 1)])
    after = lax.ppermute(raw[:AFTER], windows, [(i + 1, i) for i in range(count - 1)])
    feats = features(
        before, after, raw, taps.reshape(1, TAPS), whitening, basis.T, project, times
    )
    spikes = lax.all_gather(feats, "group", axis=0, tiled=True)
    shares, weights, tops = scores(spikes, centroids, counts)
    shares = lax.all_to_all(shares, "group", 0, 0)
    parts = sums(shares, weights, tops, spikes)
    near = [[NEAR * far + n for n in range(NEAR)] for far in range(FAR)]
    got = lax.all_to_all(parts, "lane", 0, 0, axis_index_groups=near)
    small = jax.ShapeDtypeStruct((PAY, 128), BF16)
    wide = jax.ShapeDtypeStruct((PAY, 128), F32)
    own, *sent = call(
        near_kernel, (wide, small, small, small), [VMEM], (VMEM,) * 4, moved=1_000_000
    )(got)
    took = [
        lax.ppermute(part, "lane", [(i, (i + NEAR * (d + 1)) % LANES) for i in range(LANES)])
        for d, part in enumerate(sent)
    ]
    total = call(far_kernel, wide, [VMEM] * 4, VMEM, moved=300_000)(own, *took)
    earlier = [
        lax.ppermute(total, "section", [(i, i + d) for i in range(SECTIONS - d)])
        for d in range(1, SECTIONS)
    ]
    return call(
        final_kernel,
        jax.ShapeDtypeStruct((1, 1, ROWS, FEAT), F32),
        [VMEM, VMEM, VMEM, VMEM, ANY, VMEM],
        VMEM,
        [pltpu.VMEM((ROWS, FEAT), BF16), pltpu.SemaphoreType.DMA],
        moved=600_000,
    )(total, *earlier, centroids, prior)


def solution(mesh):
    placed = (
        P(("section", "lane"), "group"),
        P(),
        P("group", None),
        P(),
        P(),
        P("group", None, None),
        P("group", "lane"),
        P(("section", "lane"), "group", None),
        P(("section", "lane"), "group"),
    )
    return jax.shard_map(
        per_device,
        mesh=mesh,
        in_specs=placed,
        out_specs=P("section", "group", "lane", None),
        check_vma=False,
    )
```

time: 286 us -> 131 us (0.46)
  the two profiles are of different devices: /device:TPU:4 before, /device:TPU:8 now
where the time goes in v1:
time: 131 us
  blocking collectives  50.5 us (39%)
  starting transfers between devices  39.9 us (30%)
  Pallas kernels  22.5 us (17%)
  waiting for transfers between devices  13.4 us (10%)
  local copies, waits for them, and re-layouts  3.63 us (3%)
    all_to_all x1, blocking collectives, per_device(): got = lax.all_to_all(parts, 'lane', 0, 0, axis_index_groups=near)  26 us
    ppermute x3, starting transfers between devices, per_device(): lax.ppermute(part, 'lane', [(i, (i + NEAR * (d + 1)) % LANES) for i in ra...  19.4 us
    all_gather x1, blocking collectives, per_device(): spikes = lax.all_gather(feats, 'group', axis=0, tiled=True)  15.1 us
    all_to_all x1, blocking collectives, per_device(): shares = lax.all_to_all(shares, 'group', 0, 0)  9.39 us
    ppermute x1, starting transfers between devices, per_device(): lax.ppermute(raw[:AFTER], windows, [(i + 1, i) for i in range(count - 1)])  9.37 us
    pallas_call x1, Pallas kernels, features(): call(features_kernel, jax.ShapeDtypeStruct((SPK, FEAT), BF16), [VMEM, VME...  7.71 us
    ppermute x3, waiting for transfers between devices, per_device(): lax.ppermute(part, 'lane', [(i, (i + NEAR * (d + 1)) % LANES) for i in ra...  7.44 us
    ppermute x3, starting transfers between devices, per_device(): lax.ppermute(total, 'section', [(i, i + d) for i in range(SECTIONS - d)])  7.29 us
  transfers between devices with their start and end apart: 8, of which 5 were waited for; matrix products, arithmetic and copies ran while one was open for 1% of the time, Pallas kernels for 0%

profile of v1, /device:TPU:8, one launch (start us, length us, event | category | flops | bytes accessed | tf_op | source)
XLA Modules:
  0.0 130.7 jit_solution(18109343710376925822)
XLA Ops:
  0.0 0.9 slice.6
  0.9 3.8 %collective-permute-start = (bf16[128,384]{1,0:T(8,128)(2,1)S(1)}, bf16[128,384]{1,0:T(8,128)(2,1)S(1)}, u32[]{:S(2)}, u32[]{:S(2)}) collective-permute-start(bf16[128,384]{1,0:T(8,128)(2,1)S(1)} %slice.6), channel_id=1, source_target_pairs={{0,8},{8,16},{16,24},{24,32},{32,40},{40,48},{48,56},{56,64},{64,7... | collective-permute-start | bytes 294920 | tf_op jit(solution)/shard_map/ppermute | solution.py:303
  4.7 0.8 slice.7
  5.5 9.4 %collective-permute-start.1 = (bf16[64,384]{1,0:T(8,128)(2,1)S(1)}, bf16[64,384]{1,0:T(8,128)(2,1)S(1)}, u32[]{:S(2)}, u32[]{:S(2)}) collective-permute-start(bf16[64,384]{1,0:T(8,128)(2,1)S(1)} %slice.7), channel_id=1, source_target_pairs={{8,0},{16,8},{24,16},{32,24},{40,32},{48,40},{56,48},{64,56},{72,6... | collective-permute-start | bytes 147464 | tf_op jit(solution)/shard_map/ppermute | solution.py:304
  15.6 1.1 collective-permute-done.1.after
  16.7 0.0 copy-start.7
  16.7 0.0 collective-permute-done.before
  16.7 0.0 copy-start.6
  16.7 0.6 copy-done.7
  17.3 0.0 copy-done.6
  17.3 7.7 %shard_map.91 = bf16[128,384]{1,0:T(8,128)(2,1)} custom-call(bf16[128,384]{1,0:T(8,128)(2,1)} %copy-done.6, bf16[64,384]{1,0:T(8,128)(2,1)} %copy-done.7, bf16[1024,384]{1,0:T(8,128)(2,1)} %raw.1, f32[1,64]{1,0:T(1,128)} %bitcast.3, bf16[384,384]{1,0:T(8,128)(2,1)} %whitening.1, bf16[6,121]{1,0:T(8,128)(2,1)} %bitcast.2, bf16[2304,384]{1,0:T(8,128)(2,1)} %project.1, ...), custom_call_target="tpu_custom_call" | custom-call | flops 2500000000 | bytes 4000000 | tf_op jit(solution)/shard_map/pallas_call | solution.py:128
  25.0 15.1 %all_gather.3.spikes = bf16[1024,384]{1,0:T(8,128)(2,1)} all-gather(bf16[128,384]{1,0:T(8,128)(2,1)} %shard_map.91), channel_id=1, replica_groups=mesh['section'=4,'lane'=16,'group'=8] {'group'}, dimensions={0}, use_global_device_ids=true | all-gather | bytes 884736 | tf_op jit(solution)/shard_map/all_gather | solution.py:308
  40.1 4.7 %shard_map.92 = (f32[8,8,128]{2,1,0:T(8,128)}, bf16[1024,1024]{1,0:T(8,128)(2,1)}, f32[8,128]{1,0:T(8,128)}) custom-call(bf16[1024,384]{1,0:T(8,128)(2,1)} %all_gather.3.spikes, bf16[1,1024,384]{2,1,0:T(8,128)(2,1)} %centers.3, s32[1,1]{1,0:T(1,128)S(6)} %copy.10.counts), custom_call_target="tpu_custom_call" | custom-call | flops 1000000000 | bytes 4000000 | tf_op jit(solution)/shard_map/pallas_call | solution.py:181
  44.8 9.4 %all_to_all.10.shares = f32[8,8,128]{2,1,0:T(8,128)} all-to-all(f32[8,8,128]{2,1,0:T(8,128)} %get-tuple-element.12), channel_id=1, replica_groups=mesh['section'=4,'lane'=16,'group'=8] {'group'}, dimensions={0} | all-to-all | bytes 65536 | tf_op jit(solution)/shard_map/all_to_all | solution.py:310
  54.2 4.0 %shard_map.93 = bf16[4,4,208,128]{3,2,1,0:T(8,128)(2,1)} custom-call(f32[8,8,128]{2,1,0:T(8,128)} %all_to_all.10.shares, bf16[1024,1024]{1,0:T(8,128)(2,1)} %get-tuple-element.13.weights, f32[8,128]{1,0:T(8,128)} %get-tuple-element.14.tops, bf16[1024,384]{1,0:T(8,128)(2,1)} %all_gather.3.spikes), custom_call_target="tpu_custom_call" | custom-call | flops 1000000000 | bytes 4000000 | tf_op jit(solution)/shard_map/pallas_call | solution.py:241
  58.2 26.0 %all_to_all.11.got = bf16[4,4,208,128]{3,2,1,0:T(8,128)(2,1)} all-to-all(bf16[4,4,208,128]{3,2,1,0:T(8,128)(2,1)} %shard_map.93), channel_id=1, replica_groups={{0,8,16,24},{32,40,48,56},{64,72,80,88},{96,104,112,120},{1,9,17,25},{3..., dimensions={0} | all-to-all | bytes 1703936 | tf_op jit(solution)/shard_map/all_to_all | solution.py:313
  84.2 1.9 %shard_map.94 = (f32[208,128]{1,0:T(8,128)}, bf16[208,128]{1,0:T(8,128)(2,1)}, bf16[208,128]{1,0:T(8,128)(2,1)}, bf16[208,128]{1,0:T(8,128)(2,1)}) custom-call(bf16[4,4,208,128]{3,2,1,0:T(8,128)(2,1)} %all_to_all.11.got), custom_call_target="tpu_custom_call" | custom-call | bytes 1000000 | tf_op jit(solution)/shard_map/pallas_call | solution.py:316
  86.1 7.8 %collective-permute-start.2 = (bf16[208,128]{1,0:T(8,128)(2,1)}, bf16[208,128]{1,0:T(8,128)(2,1)S(1)}, u32[]{:S(2)}, u32[]{:S(2)}) collective-permute-start(bf16[208,128]{1,0:T(8,128)(2,1)} %get-tuple-element.16), channel_id=1, source_target_pairs={{0,32},{8,40},{16,48},{24,56},{32,64},{40,72},{48,80},{56,88},{64,... | collective-permute-start | bytes 159752 | tf_op jit(solution)/shard_map/ppermute | solution.py:320
  93.9 6.1 %collective-permute-start.3 = (bf16[208,128]{1,0:T(8,128)(2,1)}, bf16[208,128]{1,0:T(8,128)(2,1)S(1)}, u32[]{:S(2)}, u32[]{:S(2)}) collective-permute-start(bf16[208,128]{1,0:T(8,128)(2,1)} %get-tuple-element.17), channel_id=1, source_target_pairs={{0,64},{8,72},{16,80},{24,88},{32,96},{40,104},{48,112},{56,120},{... | collective-permute-start | bytes 159752 | tf_op jit(solution)/shard_map/ppermute | solution.py:320
  100.0 5.5 %collective-permute-start.4 = (bf16[208,128]{1,0:T(8,128)(2,1)}, bf16[208,128]{1,0:T(8,128)(2,1)S(1)}, u32[]{:S(2)}, u32[]{:S(2)}) collective-permute-start(bf16[208,128]{1,0:T(8,128)(2,1)} %get-tuple-element.18), channel_id=1, source_target_pairs={{0,96},{8,104},{16,112},{24,120},{32,0},{40,8},{48,16},{56,24},{64... | collective-permute-start | bytes 159752 | tf_op jit(solution)/shard_map/ppermute | solution.py:320
  105.6 0.0 collective-permute-done.2.one
  105.6 0.0 copy-start.3
  105.6 3.9 %collective-permute-done.3.two = bf16[208,128]{1,0:T(8,128)(2,1)S(1)} collective-permute-done((bf16[208,128]{1,0:T(8,128)(2,1)}, bf16[208,128]{1,0:T(8,128)(2,1)S(1)}, u32[]{:S(2)}, u32[]{:S(2)}) %collective-permute-start.3) | collective-permute-done | bytes 53280 | tf_op jit(solution)/shard_map/ppermute | solution.py:320
  109.5 0.0 copy-start.4
  109.5 3.5 %collective-permute-done.4.three = bf16[208,128]{1,0:T(8,128)(2,1)S(1)} collective-permute-done((bf16[208,128]{1,0:T(8,128)(2,1)}, bf16[208,128]{1,0:T(8,128)(2,1)S(1)}, u32[]{:S(2)}, u32[]{:S(2)}) %collective-permute-start.4) | collective-permute-done | bytes 53280 | tf_op jit(solution)/shard_map/ppermute | solution.py:320
  113.0 0.0 copy-start.5
  113.0 0.0 copy-done.3
  113.0 0.0 copy-done.4
  113.0 0.6 copy-done.5
  113.6 1.7 %shard_map.95.own = f32[208,128]{1,0:T(8,128)} custom-call(f32[208,128]{1,0:T(8,128)} %get-tuple-element.15.own, bf16[208,128]{1,0:T(8,128)(2,1)} %copy-done.3, bf16[208,128]{1,0:T(8,128)(2,1)} %copy-done.4, bf16[208,128]{1,0:T(8,128)(2,1)} %copy-done.5), custom_call_target="tpu_custom_call" | custom-call | bytes 300000 | tf_op jit(solution)/shard_map/pallas_call | solution.py:323
  115.3 0.7 collective-permute-start.7
  116.0 4.7 %collective-permute-start.6 = (f32[208,128]{1,0:T(8,128)}, f32[208,128]{1,0:T(8,128)S(1)}, u32[]{:S(2)}, u32[]{:S(2)}) collective-permute-start(f32[208,128]{1,0:T(8,128)} %shard_map.95.own), channel_id=1, source_target_pairs={{0,256},{128,384},{1,257},{129,385},{2,258},{130,386},{3,259},{131... | collective-permute-start | bytes 319496 | tf_op jit(solution)/shard_map/ppermute | solution.py:325
  120.7 1.9 %collective-permute-start.5 = (f32[208,128]{1,0:T(8,128)}, f32[208,128]{1,0:T(8,128)S(1)}, u32[]{:S(2)}, u32[]{:S(2)}) collective-permute-start(f32[208,128]{1,0:T(8,128)} %shard_map.95.own), channel_id=1, source_target_pairs={{0,128},{128,256},{256,384},{1,129},{129,257},{257,385},{2,130},{1... | collective-permute-start | bytes 319496 | tf_op jit(solution)/shard_map/ppermute | solution.py:325
  122.6 0.0 collective-permute-done.7.three
  122.6 0.0 copy-start
  122.6 0.6 collective-permute-done.6.two
  123.3 0.0 copy-start.1
  123.3 4.2 %collective-permute-done.5.one = f32[208,128]{1,0:T(8,128)S(1)} collective-permute-done((f32[208,128]{1,0:T(8,128)}, f32[208,128]{1,0:T(8,128)S(1)}, u32[]{:S(2)}, u32[]{:S(2)}) %collective-permute-start.5) | collective-permute-done | bytes 106528 | tf_op jit(solution)/shard_map/ppermute | solution.py:325
  127.5 0.0 copy-done
  127.5 0.0 copy-done.1
  127.5 0.0 copy-start.2
  127.5 0.6 copy-done.2
  128.1 2.5 %shard_map.96 = f32[1,1,64,384]{3,2,1,0:T(8,128)} custom-call(f32[208,128]{1,0:T(8,128)} %shard_map.95.own, f32[208,128]{1,0:T(8,128)} %copy-done.2, f32[208,128]{1,0:T(8,128)} %copy-done.1, f32[208,128]{1,0:T(8,128)} %copy-done, bf16[1,1024,384]{2,1,0:T(8,128)(2,1)} %centers.3, f32[1,64]{1,0:T(1,128)} %prior.1), custom_call_target="tpu_custom_call" | custom-call | bytes 600000 | tf_op jit(solution)/shard_map/pallas_call | solution.py:328
Async XLA Ops:
  0.9 15.8 %collective-permute-start = (bf16[128,384]{1,0:T(8,128)(2,1)S(1)}, bf16[128,384]{1,0:T(8,128)(2,1)S(1)}, u32[]{:S(2)}, u32[]{:S(2)}) collective-permute-start(bf16[128,384]{1,0:T(8,128)(2,1)S(1)} %slice.6), channel_id=1, source_target_pairs={{0,8},{8,16},{16,24},{24,32},{32,40},{40,48},{48,56},{56,64},{64,7... | collective-permute-start | bytes 294920 | tf_op jit(solution)/shard_map/ppermute | solution.py:303
  5.5 11.1 %collective-permute-start.1 = (bf16[64,384]{1,0:T(8,128)(2,1)S(1)}, bf16[64,384]{1,0:T(8,128)(2,1)S(1)}, u32[]{:S(2)}, u32[]{:S(2)}) collective-permute-start(bf16[64,384]{1,0:T(8,128)(2,1)S(1)} %slice.7), channel_id=1, source_target_pairs={{8,0},{16,8},{24,16},{32,24},{40,32},{48,40},{56,48},{64,56},{72,6... | collective-permute-start | bytes 147464 | tf_op jit(solution)/shard_map/ppermute | solution.py:304
  16.7 0.6 copy-start.7
  16.7 0.7 copy-start.6
  86.1 19.4 %collective-permute-start.2 = (bf16[208,128]{1,0:T(8,128)(2,1)}, bf16[208,128]{1,0:T(8,128)(2,1)S(1)}, u32[]{:S(2)}, u32[]{:S(2)}) collective-permute-start(bf16[208,128]{1,0:T(8,128)(2,1)} %get-tuple-element.16), channel_id=1, source_target_pairs={{0,32},{8,40},{16,48},{24,56},{32,64},{40,72},{48,80},{56,88},{64,... | collective-permute-start | bytes 159752 | tf_op jit(solution)/shard_map/ppermute | solution.py:320
  93.9 15.5 %collective-permute-start.3 = (bf16[208,128]{1,0:T(8,128)(2,1)}, bf16[208,128]{1,0:T(8,128)(2,1)S(1)}, u32[]{:S(2)}, u32[]{:S(2)}) collective-permute-start(bf16[208,128]{1,0:T(8,128)(2,1)} %get-tuple-element.17), channel_id=1, source_target_pairs={{0,64},{8,72},{16,80},{24,88},{32,96},{40,104},{48,112},{56,120},{... | collective-permute-start | bytes 159752 | tf_op jit(solution)/shard_map/ppermute | solution.py:320
  100.0 13.0 %collective-permute-start.4 = (bf16[208,128]{1,0:T(8,128)(2,1)}, bf16[208,128]{1,0:T(8,128)(2,1)S(1)}, u32[]{:S(2)}, u32[]{:S(2)}) collective-permute-start(bf16[208,128]{1,0:T(8,128)(2,1)} %get-tuple-element.18), channel_id=1, source_target_pairs={{0,96},{8,104},{16,112},{24,120},{32,0},{40,8},{48,16},{56,24},{64... | collective-permute-start | bytes 159752 | tf_op jit(solution)/shard_map/ppermute | solution.py:320
  105.6 7.5 %copy-start.3 = (bf16[208,128]{1,0:T(8,128)(2,1)}, bf16[208,128]{1,0:T(8,128)(2,1)S(1)}, u32[]{:S(2)}) copy-start(bf16[208,128]{1,0:T(8,128)(2,1)S(1)} %collective-permute-done.2.one) | copy-start | bytes 159748
  109.5 3.5 %copy-start.4 = (bf16[208,128]{1,0:T(8,128)(2,1)}, bf16[208,128]{1,0:T(8,128)(2,1)S(1)}, u32[]{:S(2)}) copy-start(bf16[208,128]{1,0:T(8,128)(2,1)S(1)} %collective-permute-done.3.two) | copy-start | bytes 159748
  113.0 0.6 copy-start.5
  115.3 7.3 %collective-permute-start.7 = (f32[208,128]{1,0:T(8,128)}, f32[208,128]{1,0:T(8,128)S(1)}, u32[]{:S(2)}, u32[]{:S(2)}) collective-permute-start(f32[208,128]{1,0:T(8,128)} %shard_map.95.own), channel_id=1, source_target_pairs={{0,384},{1,385},{2,386},{3,387},{4,388},{5,389},{6,390},{7,391},{8... | collective-permute-start | bytes 319496 | tf_op jit(solution)/shard_map/ppermute | solution.py:325
  116.0 7.3 %collective-permute-start.6 = (f32[208,128]{1,0:T(8,128)}, f32[208,128]{1,0:T(8,128)S(1)}, u32[]{:S(2)}, u32[]{:S(2)}) collective-permute-start(f32[208,128]{1,0:T(8,128)} %shard_map.95.own), channel_id=1, source_target_pairs={{0,256},{128,384},{1,257},{129,385},{2,258},{130,386},{3,259},{131... | collective-permute-start | bytes 319496 | tf_op jit(solution)/shard_map/ppermute | solution.py:325
  120.7 6.8 %collective-permute-start.5 = (f32[208,128]{1,0:T(8,128)}, f32[208,128]{1,0:T(8,128)S(1)}, u32[]{:S(2)}, u32[]{:S(2)}) collective-permute-start(f32[208,128]{1,0:T(8,128)} %shard_map.95.own), channel_id=1, source_target_pairs={{0,128},{128,256},{256,384},{1,129},{129,257},{257,385},{2,130},{1... | collective-permute-start | bytes 319496 | tf_op jit(solution)/shard_map/ppermute | solution.py:325
  122.6 4.9 %copy-start = (f32[208,128]{1,0:T(8,128)}, f32[208,128]{1,0:T(8,128)S(1)}, u32[]{:S(2)}) copy-start(f32[208,128]{1,0:T(8,128)S(1)} %collective-permute-done.7.three) | copy-start | bytes 319492
  123.3 4.2 %copy-start.1 = (f32[208,128]{1,0:T(8,128)}, f32[208,128]{1,0:T(8,128)S(1)}, u32[]{:S(2)}) copy-start(f32[208,128]{1,0:T(8,128)S(1)} %collective-permute-done.6.two) | copy-start | bytes 319492
  127.5 0.6 copy-start.2

commit v2 on v1

--- a/solution.py
+++ b/solution.py
@@ -33,11 +33,14 @@
 AFTER = 64
 BLOCK = 192
 SPAN = BLOCK + TAPS
-WHITE_ROWS = 1152
 PLACE = 1280
+HEAD = 128
+LATE = 1024
+MIDDLE = 960
+EDGE = HEAD + PLACE - LATE
 PAY = 208
 SUM_ROWS = 192
-VMEM_LIMIT = 56 * 1024 * 1024
+VMEM_LIMIT = 20 * 1024 * 1024
 
 VMEM = pl.BlockSpec(memory_space=pltpu.VMEM)
 SMEM = pl.BlockSpec(memory_space=pltpu.SMEM)
@@ -56,15 +59,10 @@
     )
 
 
-def features_kernel(
-    before, after, raw, taps, whitening, basis, project, times, out,
-    window, band, row, snip, white, place, comps, flat, held, raw_sem, project_sem,
+def inner_kernel(
+    raw, taps, whitening, basis, times, found, middle, place, band,
+    row, snip, rows,
 ):
-    raw_copy = pltpu.make_async_copy(raw, window.at[pl.ds(BEFORE, SEG)], raw_sem)
-    raw_copy.start()
-    project_copy = pltpu.make_async_copy(project, held, project_sem)
-    project_copy.start()
-
     row[...] = jnp.zeros_like(row)
     row[0:1, 0:TAPS] = taps[...]
     spread = jnp.broadcast_to(row[0:1, :], (SPAN, SPAN))
@@ -76,76 +74,109 @@
 
     snip[...] = jnp.zeros_like(snip)
     snip[0:RANKS, 0:SNIP] = basis[...].astype(F32)
-
-    def clear(i, carry):
-        place[pl.ds(pl.multiple_of(i * 32, 32), 32), :] = jnp.zeros((32, PLACE), F32)
-        return carry
-
-    lax.fori_loop(0, SPK * 8 // 32, clear, 0)
     shape = snip[...]
+    rows[...] = jnp.zeros_like(rows)
 
     def put(s, carry):
         u = times[0, 0, s] + (64 - HALF)
         start = pl.multiple_of((u >> 7) * 128, 128)
         at = pl.multiple_of(s * 8, 8)
-        place[pl.ds(at, 8), pl.ds(start, 256)] = pltpu.roll(shape, u & 127, 1)
+        rows[pl.ds(at, 8), pl.ds(start, 256)] = pltpu.roll(shape, u & 127, 1)
         return carry
 
     lax.fori_loop(0, SPK, put, 0, unroll=8)
 
-    window[0:BEFORE, :] = before[...]
-    window[BEFORE + SEG : BEFORE + SEG + AFTER, :] = after[...]
-    raw_copy.wait()
-    for b in range(WHITE_ROWS // BLOCK):
-        rows = window[b * BLOCK : b * BLOCK + SPAN, :]
-        both = jnp.dot(band[...], rows, preferred_element_type=F32)
+    for b in range(5):
+        both = jnp.dot(
+            band[...], raw[b * BLOCK : b * BLOCK + SPAN, :], preferred_element_type=F32
+        )
         trace = (both[0:BLOCK] + both[BLOCK : 2 * BLOCK]).astype(BF16)
-        white[b * BLOCK : (b + 1) * BLOCK, :] = jnp.dot(
+        middle[b * BLOCK : (b + 1) * BLOCK, :] = jnp.dot(
             trace, whitening[...], preferred_element_type=F32
         ).astype(BF16)
-    white[WHITE_ROWS:PLACE, :] = jnp.zeros((PLACE - WHITE_ROWS, CH), BF16)
+    for c in range(4):
+        part = slice(c * 256, (c + 1) * 256)
+        place[part, 0:HEAD] = rows[part, 0:HEAD].astype(BF16)
+        place[part, HEAD:EDGE] = rows[part, LATE:PLACE].astype(BF16)
+        found[part, :] = jnp.dot(
+            rows[part, HEAD:LATE].astype(BF16), middle[0 : LATE - HEAD, :],
+            preferred_element_type=F32,
+        )
+
+
+def inner(raw, taps, whitening, basis, times):
+    return call(
+        inner_kernel,
+        (
+            jax.ShapeDtypeStruct((SPK * 8, CH), F32),
+            jax.ShapeDtypeStruct((MIDDLE, CH), BF16),
+            jax.ShapeDtypeStruct((SPK * 8, EDGE), BF16),
+            jax.ShapeDtypeStruct((2 * BLOCK, SPAN), BF16),
+        ),
+        [VMEM, VMEM, VMEM, VMEM, SMEM],
+        (VMEM, VMEM, VMEM, VMEM),
+        [
+            pltpu.VMEM((8, SPAN), F32),
+            pltpu.VMEM((8, 256), F32),
+            pltpu.VMEM((SPK * 8, PLACE), F32),
+        ],
+        flops=2_000_000_000,
+        moved=6_000_000,
+    )(raw, taps, whitening, basis, times)
+
+
+def features_kernel(
+    before, after, raw, whitening, found, middle, place, band, project, out,
+    window, white, comps, flat,
+):
+    window[0:BEFORE, :] = before[...]
+    window[BEFORE:SPAN, :] = raw[0 : SPAN - BEFORE, :]
+    window[SPAN : 2 * SPAN - AFTER, :] = raw[SEG - SPAN + AFTER : SEG, :]
+    window[2 * SPAN - AFTER : 2 * SPAN, :] = after[...]
+    for b in range(2):
+        both = jnp.dot(band[...], window[b * SPAN : (b + 1) * SPAN, :], preferred_element_type=F32)
+        trace = (both[0:BLOCK] + both[BLOCK : 2 * BLOCK]).astype(BF16)
+        fresh = jnp.dot(trace, whitening[...], preferred_element_type=F32).astype(BF16)
+        if b == 0:
+            white[0:HEAD, :] = fresh[0:HEAD]
+        else:
+            white[HEAD + 64 : HEAD + 128, :] = fresh[BLOCK - 64 : BLOCK]
+    white[HEAD : HEAD + 64, :] = middle[LATE - HEAD : MIDDLE, :]
+    white[HEAD + 128 : EDGE, :] = jnp.zeros((EDGE - HEAD - 128, CH), BF16)
     last = (lax.axis_index("section") == SECTIONS - 1) & (lax.axis_index("lane") == LANES - 1)
 
     @pl.when(last)
     def _():
-        white[64 + SEG : WHITE_ROWS, :] = jnp.zeros((WHITE_ROWS - 64 - SEG, CH), BF16)
+        white[HEAD + 64 : HEAD + 128, :] = jnp.zeros((64, CH), BF16)
 
     for c in range(4):
-        part = place[c * 256 : (c + 1) * 256, :].astype(BF16)
-        found = jnp.dot(part, white[...], preferred_element_type=F32)
+        part = slice(c * 256, (c + 1) * 256)
+        whole = found[part, :] + jnp.dot(place[part, :], white[...], preferred_element_type=F32)
         for i in range(CH // 128):
-            comps[i, c * 256 : (c + 1) * 256, :] = found[:, i * 128 : (i + 1) * 128]
+            comps[i, part, :] = whole[:, i * 128 : (i + 1) * 128]
     for r in range(RANKS):
         for i in range(CH // 128):
             flat[:, r * CH + i * 128 : r * CH + (i + 1) * 128] = comps[
                 i, pl.ds(r, SPK, stride=8), :
             ].astype(BF16)
-    project_copy.wait()
-    out[...] = jnp.dot(flat[...], held[...], preferred_element_type=F32).astype(BF16)
-
-
-def features(before, after, raw, taps, whitening, basis, project, times):
+    out[...] = jnp.dot(flat[...], project[...], preferred_element_type=F32).astype(BF16)
+
+
+def features(before, after, raw, whitening, found, middle, place, band, project):
     return call(
         features_kernel,
         jax.ShapeDtypeStruct((SPK, FEAT), BF16),
-        [VMEM, VMEM, ANY, VMEM, VMEM, VMEM, ANY, SMEM],
+        [VMEM] * 9,
         VMEM,
         [
-            pltpu.VMEM((BEFORE + SEG + AFTER, CH), BF16),
-            pltpu.VMEM((2 * BLOCK, SPAN), BF16),
-            pltpu.VMEM((8, SPAN), F32),
-            pltpu.VMEM((8, 256), F32),
-            pltpu.VMEM((PLACE, CH), BF16),
-            pltpu.VMEM((SPK * 8, PLACE), F32),
+            pltpu.VMEM((2 * SPAN, CH), BF16),
+            pltpu.VMEM((EDGE, CH), BF16),
             pltpu.VMEM((CH // 128, SPK * 8, 128), F32),
             pltpu.VMEM((SPK, RANKS * CH), BF16),
-            pltpu.VMEM((RANKS * CH, FEAT), BF16),
-            pltpu.SemaphoreType.DMA,
-            pltpu.SemaphoreType.DMA,
         ],
-        flops=2_500_000_000,
-        moved=4_000_000,
-    )(before, after, raw, taps, whitening, basis, project, times)
+        flops=1_000_000_000,
+        moved=6_000_000,
+    )(before, after, raw, whitening, found, middle, place, band, project)
 
 
 def scores_kernel(spikes, centers, counts, shares, weights, tops, logits):
@@ -302,9 +333,8 @@
     count = SECTIONS * LANES
     before = lax.ppermute(raw[SEG - BEFORE :], windows, [(i, i + 1) for i in range(count - 1)])
     after = lax.ppermute(raw[:AFTER], windows, [(i + 1, i) for i in range(count - 1)])
-    feats = features(
-        before, after, raw, taps.reshape(1, TAPS), whitening, basis.T, project, times
-    )
+    held = inner(raw, taps.reshape(1, TAPS), whitening, basis.T, times)
+    feats = features(before, after, raw, whitening, *held, project)
     spikes = lax.all_gather(feats, "group", axis=0, tiled=True)
     shares, weights, tops = scores(spikes, centroids, counts)
     shares = lax.all_to_all(shares, "group", 0, 0)

time: 131 us -> 115 us (0.88)
  Pallas kernels: 22.5 us -> 11.4 us
  blocking collectives: 50.5 us -> 46.9 us
  local copies, waits for them, and re-layouts: 3.63 us -> 5.81 us
  waiting for transfers between devices: 13.4 us -> 11.7 us
  starting transfers between devices: 39.9 us -> 38.3 us
    pallas_call x1, Pallas kernels: 3.98 us -> 1.28 us  [sums(): call(sums_kernel, jax.ShapeDtypeStruct((NEAR, FAR, PAY, 128), BF16), [VME...]
    pallas_call x1, Pallas kernels: 4.68 us -> 1.98 us  [scores(): call(scores_kernel, (jax.ShapeDtypeStruct((GROUP, GROUP, SPK), F32), jax....]
    unnamed x16, local copies, waits for them, and re-layouts: 1.92 us -> 4.1 us
    ppermute x1, starting transfers between devices: 3.83 us -> 1.92 us  [per_device(): lax.ppermute(raw[SEG - BEFORE:], windows, [(i, i + 1) for i in range(coun...]
    ppermute x1, starting transfers between devices: 9.37 us -> 11.3 us  [per_device(): lax.ppermute(raw[:AFTER], windows, [(i + 1, i) for i in range(count - 1)])]
    all_to_all x1, blocking collectives: 26 us -> 24.1 us  [per_device(): got = lax.all_to_all(parts, 'lane', 0, 0, axis_index_groups=near)]
    ppermute x3, starting transfers between devices: 7.29 us -> 5.46 us  [per_device(): lax.ppermute(total, 'section', [(i, i + d) for i in range(SECTIONS - d)])]
    pallas_call x1, Pallas kernels: 1.94 us -> 0.11 us  [per_device(): call(near_kernel, (wide, small, small, small), [VMEM], (VMEM,) * 4, moved...]
  transfers between devices with their start and end apart: 8 -> 8, of which waited for: 5 -> 4; matrix products, arithmetic and copies ran while one was open for 1% -> 1% of each run, Pallas kernels for 0% -> 5%
where the time goes in v2:
time: 115 us
  blocking collectives  46.9 us (41%)
  starting transfers between devices  38.3 us (33%)
  waiting for transfers between devices  11.7 us (10%)
  Pallas kernels  11.4 us (10%)
  local copies, waits for them, and re-layouts  5.81 us (5%)
    all_to_all x1, blocking collectives, per_device(): got = lax.all_to_all(parts, 'lane', 0, 0, axis_index_groups=near)  24.1 us
    ppermute x3, starting transfers between devices, per_device(): lax.ppermute(part, 'lane', [(i, (i + NEAR * (d + 1)) % LANES) for i in ra...  19.6 us
    all_gather x1, blocking collectives, per_device(): spikes = lax.all_gather(feats, 'group', axis=0, tiled=True)  13.7 us
    ppermute x1, starting transfers between devices, per_device(): lax.ppermute(raw[:AFTER], windows, [(i + 1, i) for i in range(count - 1)])  11.3 us
    all_to_all x1, blocking collectives, per_device(): shares = lax.all_to_all(shares, 'group', 0, 0)  9.03 us
    ppermute x3, waiting for transfers between devices, per_device(): lax.ppermute(part, 'lane', [(i, (i + NEAR * (d + 1)) % LANES) for i in ra...  6.93 us
    ppermute x3, starting transfers between devices, per_device(): lax.ppermute(total, 'section', [(i, i + d) for i in range(SECTIONS - d)])  5.46 us
    pallas_call x1, Pallas kernels, inner(): call(inner_kernel, (jax.ShapeDtypeStruct((SPK * 8, CH), F32), jax.ShapeDt...  5.23 us
  transfers between devices with their start and end apart: 8, of which 4 were waited for; matrix products, arithmetic and copies ran while one was open for 1% of the time, Pallas kernels for 5%

profile of v2, /device:TPU:8, one launch (start us, length us, event | category | flops | bytes accessed | tf_op | source)
XLA Modules:
  0.0 114.8 jit_solution(5219386796717076813)
XLA Ops:
  0.0 0.8 slice.7
  0.8 11.3 %collective-permute-start.1 = (bf16[64,384]{1,0:T(8,128)(2,1)S(1)}, bf16[64,384]{1,0:T(8,128)(2,1)S(1)}, u32[]{:S(2)}, u32[]{:S(2)}) collective-permute-start(bf16[64,384]{1,0:T(8,128)(2,1)S(1)} %slice.7), channel_id=1, source_target_pairs={{8,0},{16,8},{24,16},{32,24},{40,32},{48,40},{56,48},{64,56},{72,6... | collective-permute-start | bytes 147464 | tf_op jit(solution)/shard_map/ppermute | solution.py:335
  12.1 0.9 slice.6
  13.0 1.9 %collective-permute-start = (bf16[128,384]{1,0:T(8,128)(2,1)S(1)}, bf16[128,384]{1,0:T(8,128)(2,1)S(1)}, u32[]{:S(2)}, u32[]{:S(2)}) collective-permute-start(bf16[128,384]{1,0:T(8,128)(2,1)S(1)} %slice.6), channel_id=1, source_target_pairs={{0,8},{8,16},{16,24},{24,32},{32,40},{40,48},{48,56},{56,64},{64,7... | collective-permute-start | bytes 294920 | tf_op jit(solution)/shard_map/ppermute | solution.py:334
  14.9 0.0 copy-start.1
  14.9 1.1 copy-done.1
  16.1 0.0 copy-start.3
  16.1 1.0 copy-done.3
  17.0 0.0 copy-start.5
  17.0 0.7 copy-done.5
  17.7 0.0 copy-start.6
  17.7 0.7 copy-done.6
  18.4 0.0 copy-start.7
  18.4 0.7 copy-done.7
  19.0 0.0 copy-start
  19.0 5.2 %shard_map.91 = (f32[1024,384]{1,0:T(8,128)S(1)}, bf16[960,384]{1,0:T(8,128)(2,1)S(1)}, bf16[1024,384]{1,0:T(8,128)(2,1)S(1)}, bf16[384,256]{1,0:T(8,128)(2,1)S(1)}) custom-call(bf16[1024,384]{1,0:T(8,128)(2,1)S(1)} %copy-done.1, f32[1,64]{1,0:T(1,128)S(1)} %bitcast.3, bf16[384,384]{1,0:T(8,128)(2,1)S(1)} %copy-done.3, bf16[6,121]{1,0:T(8,128)(2,1)S(1)} %bitcast.2, ...), custom_call_target="tpu_custom_call" | custom-call | flops 2000000000 | bytes 6000000 | tf_op jit(solution)/shard_map/pallas_call | solution.py:108
  24.9 0.0 collective-permute-done.1.after
  24.9 0.0 collective-permute-done.before
  24.9 0.0 copy-done
  24.9 0.0 copy-start.2
  25.0 1.9 %shard_map.92 = bf16[128,384]{1,0:T(8,128)(2,1)S(1)} custom-call(bf16[128,384]{1,0:T(8,128)(2,1)S(1)} %collective-permute-done.before, bf16[64,384]{1,0:T(8,128)(2,1)S(1)} %collective-permute-done.1.after, bf16[1024,384]{1,0:T(8,128)(2,1)S(1)} %copy-done.1, bf16[384,384]{1,0:T(8,128)(2,1)S(1)} %copy-done.3, f32[1024,384]{1,0:T(8,128)S(1)} %get-tuple-element.16.found, ...), custom_call_target="tpu_custom_call" | custom-call | flops 1000000000 | bytes 6000000 | tf_op jit(solution)/shard_map/pallas_call | solution.py:166
  26.8 13.7 %all_gather.3.spikes = bf16[1024,384]{1,0:T(8,128)(2,1)S(1)} all-gather(bf16[128,384]{1,0:T(8,128)(2,1)S(1)} %shard_map.92), channel_id=1, replica_groups=mesh['section'=4,'lane'=16,'group'=8] {'group'}, dimensions={0}, use_global_device_ids=true | all-gather | bytes 884736 | tf_op jit(solution)/shard_map/all_gather | solution.py:338
  40.6 0.0 copy-done.2
  40.6 2.0 %shard_map.93 = (f32[8,8,128]{2,1,0:T(8,128)S(1)}, bf16[1024,1024]{1,0:T(8,128)(2,1)S(1)}, f32[8,128]{1,0:T(8,128)S(1)}) custom-call(bf16[1024,384]{1,0:T(8,128)(2,1)S(1)} %all_gather.3.spikes, bf16[1,1024,384]{2,1,0:T(8,128)(2,1)S(1)} %copy-done.2, s32[1,1]{1,0:T(1,128)S(6)} %copy.10.counts), custom_call_target="tpu_custom_call" | custom-call | flops 1000000000 | bytes 4000000 | tf_op jit(solution)/shard_map/pallas_call | solution.py:212
  42.5 9.0 %all_to_all.10.shares = f32[8,8,128]{2,1,0:T(8,128)S(1)} all-to-all(f32[8,8,128]{2,1,0:T(8,128)S(1)} %get-tuple-element.20), channel_id=1, replica_groups=mesh['section'=4,'lane'=16,'group'=8] {'group'}, dimensions={0} | all-to-all | bytes 65536 | tf_op jit(solution)/shard_map/all_to_all | solution.py:340
  51.6 1.3 %shard_map.94 = bf16[4,4,208,128]{3,2,1,0:T(8,128)(2,1)S(1)} custom-call(f32[8,8,128]{2,1,0:T(8,128)S(1)} %all_to_all.10.shares, bf16[1024,1024]{1,0:T(8,128)(2,1)S(1)} %get-tuple-element.21.weights, f32[8,128]{1,0:T(8,128)S(1)} %get-tuple-element.22.tops, bf16[1024,384]{1,0:T(8,128)(2,1)S(1)} %all_gather.3.spikes), custom_call_target="tpu_custom_call" | custom-call | flops 1000000000 | bytes 4000000 | tf_op jit(solution)/shard_map/pallas_call | solution.py:272
  52.9 0.0 copy-start.4
  52.9 24.1 %all_to_all.11.got = bf16[4,4,208,128]{3,2,1,0:T(8,128)(2,1)S(1)} all-to-all(bf16[4,4,208,128]{3,2,1,0:T(8,128)(2,1)S(1)} %shard_map.94), channel_id=1, replica_groups={{0,8,16,24},{32,40,48,56},{64,72,80,88},{96,104,112,120},{1,9,17,25},{3..., dimensions={0} | all-to-all | bytes 1703936 | tf_op jit(solution)/shard_map/all_to_all | solution.py:343
  77.0 0.1 shard_map.95
  77.1 5.9 %collective-permute-start.2 = (bf16[208,128]{1,0:T(8,128)(2,1)S(1)}, bf16[208,128]{1,0:T(8,128)(2,1)S(1)}, u32[]{:S(2)}, u32[]{:S(2)}) collective-permute-start(bf16[208,128]{1,0:T(8,128)(2,1)S(1)} %get-tuple-element.24), channel_id=1, source_target_pairs={{0,32},{8,40},{16,48},{24,56},{32,64},{40,72},{48,80},{56,88},{64,... | collective-permute-start | bytes 159752 | tf_op jit(solution)/shard_map/ppermute | solution.py:350
  83.1 9.1 %collective-permute-start.3 = (bf16[208,128]{1,0:T(8,128)(2,1)S(1)}, bf16[208,128]{1,0:T(8,128)(2,1)S(1)}, u32[]{:S(2)}, u32[]{:S(2)}) collective-permute-start(bf16[208,128]{1,0:T(8,128)(2,1)S(1)} %get-tuple-element.25), channel_id=1, source_target_pairs={{0,64},{8,72},{16,80},{24,88},{32,96},{40,104},{48,112},{56,120},{... | collective-permute-start | bytes 159752 | tf_op jit(solution)/shard_map/ppermute | solution.py:350
  92.2 4.5 %collective-permute-start.4 = (bf16[208,128]{1,0:T(8,128)(2,1)S(1)}, bf16[208,128]{1,0:T(8,128)(2,1)S(1)}, u32[]{:S(2)}, u32[]{:S(2)}) collective-permute-start(bf16[208,128]{1,0:T(8,128)(2,1)S(1)} %get-tuple-element.26), channel_id=1, source_target_pairs={{0,96},{8,104},{16,112},{24,120},{32,0},{40,8},{48,16},{56,24},{64... | collective-permute-start | bytes 159752 | tf_op jit(solution)/shard_map/ppermute | solution.py:350
  96.8 0.0 collective-permute-done.2.one
  96.8 1.5 %collective-permute-done.3.two = bf16[208,128]{1,0:T(8,128)(2,1)S(1)} collective-permute-done((bf16[208,128]{1,0:T(8,128)(2,1)S(1)}, bf16[208,128]{1,0:T(8,128)(2,1)S(1)}, u32[]{:S(2)}, u32[]{:S(2)}) %collective-permute-start.3) | collective-permute-done | bytes 53280 | tf_op jit(solution)/shard_map/ppermute | solution.py:350
  98.2 5.5 %collective-permute-done.4.three = bf16[208,128]{1,0:T(8,128)(2,1)S(1)} collective-permute-done((bf16[208,128]{1,0:T(8,128)(2,1)S(1)}, bf16[208,128]{1,0:T(8,128)(2,1)S(1)}, u32[]{:S(2)}, u32[]{:S(2)}) %collective-permute-start.4) | collective-permute-done | bytes 53280 | tf_op jit(solution)/shard_map/ppermute | solution.py:350
  103.7 0.1 shard_map.96.own
  103.8 0.7 collective-permute-start.7
  104.4 2.9 %collective-permute-start.6 = (f32[208,128]{1,0:T(8,128)S(1)}, f32[208,128]{1,0:T(8,128)S(1)}, u32[]{:S(2)}, u32[]{:S(2)}) collective-permute-start(f32[208,128]{1,0:T(8,128)S(1)} %shard_map.96.own), channel_id=1, source_target_pairs={{0,256},{128,384},{1,257},{129,385},{2,258},{130,386},{3,259},{131... | collective-permute-start | bytes 319496 | tf_op jit(solution)/shard_map/ppermute | solution.py:355
  107.3 1.9 %collective-permute-start.5 = (f32[208,128]{1,0:T(8,128)S(1)}, f32[208,128]{1,0:T(8,128)S(1)}, u32[]{:S(2)}, u32[]{:S(2)}) collective-permute-start(f32[208,128]{1,0:T(8,128)S(1)} %shard_map.96.own), channel_id=1, source_target_pairs={{0,128},{128,256},{256,384},{1,129},{129,257},{257,385},{2,130},{1... | collective-permute-start | bytes 319496 | tf_op jit(solution)/shard_map/ppermute | solution.py:355
  109.2 0.0 collective-permute-done.7.three
  109.3 0.3 collective-permute-done.6.two
  109.6 4.4 %collective-permute-done.5.one = f32[208,128]{1,0:T(8,128)S(1)} collective-permute-done((f32[208,128]{1,0:T(8,128)S(1)}, f32[208,128]{1,0:T(8,128)S(1)}, u32[]{:S(2)}, u32[]{:S(2)}) %collective-permute-start.5) | collective-permute-done | bytes 106528 | tf_op jit(solution)/shard_map/ppermute | solution.py:355
  114.0 0.0 copy-done.4
  114.0 0.8 shard_map.97
Async XLA Ops:
  0.8 24.1 %collective-permute-start.1 = (bf16[64,384]{1,0:T(8,128)(2,1)S(1)}, bf16[64,384]{1,0:T(8,128)(2,1)S(1)}, u32[]{:S(2)}, u32[]{:S(2)}) collective-permute-start(bf16[64,384]{1,0:T(8,128)(2,1)S(1)} %slice.7), channel_id=1, source_target_pairs={{8,0},{16,8},{24,16},{32,24},{40,32},{48,40},{56,48},{64,56},{72,6... | collective-permute-start | bytes 147464 | tf_op jit(solution)/shard_map/ppermute | solution.py:335
  13.0 11.9 %collective-permute-start = (bf16[128,384]{1,0:T(8,128)(2,1)S(1)}, bf16[128,384]{1,0:T(8,128)(2,1)S(1)}, u32[]{:S(2)}, u32[]{:S(2)}) collective-permute-start(bf16[128,384]{1,0:T(8,128)(2,1)S(1)} %slice.6), channel_id=1, source_target_pairs={{0,8},{8,16},{16,24},{24,32},{32,40},{40,48},{48,56},{56,64},{64,7... | collective-permute-start | bytes 294920 | tf_op jit(solution)/shard_map/ppermute | solution.py:334
  14.9 1.1 copy-start.1
  16.1 1.0 copy-start.3
  17.0 0.7 copy-start.5
  17.7 0.7 copy-start.6
  18.4 0.7 copy-start.7
  19.0 5.9 %copy-start = (bf16[2304,384]{1,0:T(8,128)(2,1)S(1)}, bf16[2304,384]{1,0:T(8,128)(2,1)}, u32[]{:S(2)}) copy-start(bf16[2304,384]{1,0:T(8,128)(2,1)} %project.1) | copy-start | bytes 5308420
  24.9 15.6 %copy-start.2 = (bf16[1,1024,384]{2,1,0:T(8,128)(2,1)S(1)}, bf16[1,1024,384]{2,1,0:T(8,128)(2,1)}, u32[]{:S(2)}) copy-start(bf16[1,1024,384]{2,1,0:T(8,128)(2,1)} %centers.3) | copy-start | bytes 2359300
  52.9 61.1 %copy-start.4 = (f32[1,64]{1,0:T(1,128)S(1)}, f32[1,64]{1,0:T(1,128)}, u32[]{:S(2)}) copy-start(f32[1,64]{1,0:T(1,128)} %prior.1) | copy-start | bytes 772
  77.1 19.6 %collective-permute-start.2 = (bf16[208,128]{1,0:T(8,128)(2,1)S(1)}, bf16[208,128]{1,0:T(8,128)(2,1)S(1)}, u32[]{:S(2)}, u32[]{:S(2)}) collective-permute-start(bf16[208,128]{1,0:T(8,128)(2,1)S(1)} %get-tuple-element.24), channel_id=1, source_target_pairs={{0,32},{8,40},{16,48},{24,56},{32,64},{40,72},{48,80},{56,88},{64,... | collective-permute-start | bytes 159752 | tf_op jit(solution)/shard_map/ppermute | solution.py:350
  83.1 15.2 %collective-permute-start.3 = (bf16[208,128]{1,0:T(8,128)(2,1)S(1)}, bf16[208,128]{1,0:T(8,128)(2,1)S(1)}, u32[]{:S(2)}, u32[]{:S(2)}) collective-permute-start(bf16[208,128]{1,0:T(8,128)(2,1)S(1)} %get-tuple-element.25), channel_id=1, source_target_pairs={{0,64},{8,72},{16,80},{24,88},{32,96},{40,104},{48,112},{56,120},{... | collective-permute-start | bytes 159752 | tf_op jit(solution)/shard_map/ppermute | solution.py:350
  92.2 11.5 %collective-permute-start.4 = (bf16[208,128]{1,0:T(8,128)(2,1)S(1)}, bf16[208,128]{1,0:T(8,128)(2,1)S(1)}, u32[]{:S(2)}, u32[]{:S(2)}) collective-permute-start(bf16[208,128]{1,0:T(8,128)(2,1)S(1)} %get-tuple-element.26), channel_id=1, source_target_pairs={{0,96},{8,104},{16,112},{24,120},{32,0},{40,8},{48,16},{56,24},{64... | collective-permute-start | bytes 159752 | tf_op jit(solution)/shard_map/ppermute | solution.py:350
  103.8 5.5 %collective-permute-start.7 = (f32[208,128]{1,0:T(8,128)S(1)}, f32[208,128]{1,0:T(8,128)S(1)}, u32[]{:S(2)}, u32[]{:S(2)}) collective-permute-start(f32[208,128]{1,0:T(8,128)S(1)} %shard_map.96.own), channel_id=1, source_target_pairs={{0,384},{1,385},{2,386},{3,387},{4,388},{5,389},{6,390},{7,391},{8... | collective-permute-start | bytes 319496 | tf_op jit(solution)/shard_map/ppermute | solution.py:355
  104.4 5.2 %collective-permute-start.6 = (f32[208,128]{1,0:T(8,128)S(1)}, f32[208,128]{1,0:T(8,128)S(1)}, u32[]{:S(2)}, u32[]{:S(2)}) collective-permute-start(f32[208,128]{1,0:T(8,128)S(1)} %shard_map.96.own), channel_id=1, source_target_pairs={{0,256},{128,384},{1,257},{129,385},{2,258},{130,386},{3,259},{131... | collective-permute-start | bytes 319496 | tf_op jit(solution)/shard_map/ppermute | solution.py:355
  107.3 6.7 %collective-permute-start.5 = (f32[208,128]{1,0:T(8,128)S(1)}, f32[208,128]{1,0:T(8,128)S(1)}, u32[]{:S(2)}, u32[]{:S(2)}) collective-permute-start(f32[208,128]{1,0:T(8,128)S(1)} %shard_map.96.own), channel_id=1, source_target_pairs={{0,128},{128,256},{256,384},{1,129},{129,257},{257,385},{2,130},{1... | collective-permute-start | bytes 319496 | tf_op jit(solution)/shard_map/ppermute | solution.py:355

commit v3 on v2

--- a/solution.py
+++ b/solution.py
@@ -40,6 +40,7 @@
 EDGE = HEAD + PLACE - LATE
 PAY = 208
 SUM_ROWS = 192
+NEAR_ROWS = FAR * SUM_ROWS + 16
 VMEM_LIMIT = 20 * 1024 * 1024
 
 VMEM = pl.BlockSpec(memory_space=pltpu.VMEM)
@@ -57,6 +58,11 @@
         compiler_params=pltpu.CompilerParams(vmem_limit_bytes=VMEM_LIMIT),
         cost_estimate=pl.CostEstimate(flops=flops, bytes_accessed=moved, transcendentals=0),
     )
+
+
+def edges_kernel(raw, head, tail):
+    head[...] = raw[0:AFTER, :]
+    tail[...] = raw[SEG - BEFORE : SEG, :]
 
 
 def inner_kernel(
@@ -237,6 +243,7 @@
     lane = lax.broadcasted_iota(jnp.int32, (ROWS, 128), 1)
     pick = row == (lane & (ROWS - 1))
     front = lax.broadcasted_iota(jnp.int32, (1, 128), 1) < ROWS
+    masses = [[] for _ in range(NEAR)]
     for k in range(4):
         acc = None
         for b in range(4):
@@ -254,11 +261,17 @@
             far, near = owner // NEAR, owner % NEAR
             rows = acc[i * ROWS : (i + 1) * ROWS, :]
             for c in range(3):
-                out[near, far, c * ROWS : (c + 1) * ROWS, :] = rows[
-                    :, c * 128 : (c + 1) * 128
-                ].astype(BF16)
+                start = far * SUM_ROWS + c * ROWS
+                out[near, start : start + ROWS, :] = rows[:, c * 128 : (c + 1) * 128].astype(BF16)
             mass = jnp.sum(jnp.where(pick, rows[:, 384:512], 0.0), axis=0, keepdims=True)
-            out[near, far, SUM_ROWS:PAY, :] = split(mass, front)
+            masses[near].append(mass)
+    slot = lax.broadcasted_iota(jnp.int32, (16, 128), 0)
+    for near in range(NEAR):
+        block = jnp.zeros((16, 128), F32)
+        for far in range(FAR):
+            block = jnp.where(slot == far, jnp.broadcast_to(masses[near][far], (16, 128)), block)
+        high = block.astype(BF16).astype(F32)
+        out[near, FAR * SUM_ROWS : NEAR_ROWS, :] = jnp.where(front, high, block - high).astype(BF16)
 
 
 def split(mass, front):
@@ -271,7 +284,7 @@
 def sums(shares, weights, tops, spikes):
     return call(
         sums_kernel,
-        jax.ShapeDtypeStruct((NEAR, FAR, PAY, 128), BF16),
+        jax.ShapeDtypeStruct((NEAR, NEAR_ROWS, 128), BF16),
         [VMEM] * 4,
         VMEM,
         flops=1_000_000_000,
@@ -281,26 +294,36 @@
 
 def near_kernel(got, own, one, two, three):
     front = lax.broadcasted_iota(jnp.int32, (1, 128), 1) < ROWS
+    slot = lax.broadcasted_iota(jnp.int32, (16, 128), 0)
     mine = lax.axis_index("lane") // NEAR
+    tails = got[0, FAR * SUM_ROWS : NEAR_ROWS, :].astype(F32)
+    for n in range(1, NEAR):
+        tails = tails + got[n, FAR * SUM_ROWS : NEAR_ROWS, :].astype(F32)
     for d, out in enumerate((own, one, two, three)):
         far = lax.rem(mine + d, FAR)
-        acc = got[0, far].astype(F32)
+        part = pl.ds(pl.multiple_of(far * SUM_ROWS, 64), SUM_ROWS)
+        acc = got[0, part, :].astype(F32)
         for n in range(1, NEAR):
-            acc = acc + got[n, far].astype(F32)
-        tail = acc[SUM_ROWS : SUM_ROWS + 1, :]
+            acc = acc + got[n, part, :].astype(F32)
+        tail = jnp.sum(jnp.where(slot == far, tails, 0.0), axis=0, keepdims=True)
         mass = tail + pltpu.roll(tail, ROWS, 1)
-        out[0:SUM_ROWS, :] = acc[0:SUM_ROWS].astype(out.dtype)
+        out[0:SUM_ROWS, :] = acc.astype(out.dtype)
         if d == 0:
             out[SUM_ROWS:PAY, :] = jnp.broadcast_to(mass, (PAY - SUM_ROWS, 128))
         else:
             out[SUM_ROWS:PAY, :] = split(mass, front)
 
 
-def far_kernel(own, one, two, three, out):
+def far_kernel(own, one, two, three, out, sent):
+    front = lax.broadcasted_iota(jnp.int32, (1, 128), 1) < ROWS
     acc = one[...].astype(F32) + two[...].astype(F32) + three[...].astype(F32)
+    total = own[0:SUM_ROWS, :] + acc[0:SUM_ROWS]
     tail = acc[SUM_ROWS:PAY, :]
-    out[0:SUM_ROWS, :] = own[0:SUM_ROWS, :] + acc[0:SUM_ROWS]
-    out[SUM_ROWS:PAY, :] = own[SUM_ROWS:PAY, :] + tail + pltpu.roll(tail, ROWS, 1)
+    mass = own[SUM_ROWS:PAY, :] + tail + pltpu.roll(tail, ROWS, 1)
+    out[0:SUM_ROWS, :] = total
+    out[SUM_ROWS:PAY, :] = mass
+    sent[0:SUM_ROWS, :] = total.astype(BF16)
+    sent[SUM_ROWS:PAY, :] = split(mass[0:1], front)
 
 
 def final_kernel(own, one, two, three, centers, prior, out, held, sem):
@@ -309,7 +332,10 @@
         centers.at[0, pl.ds(pl.multiple_of(lane_at * ROWS, ROWS), ROWS)], held, sem
     )
     copy.start()
-    acc = own[...] + one[...] + two[...] + three[...]
+    past = one[...].astype(F32) + two[...].astype(F32) + three[...].astype(F32)
+    acc = own[0:SUM_ROWS, :] + past[0:SUM_ROWS]
+    tail = past[SUM_ROWS : SUM_ROWS + 1, :]
+    mass = own[SUM_ROWS : SUM_ROWS + 1, :] + tail + pltpu.roll(tail, ROWS, 1)
     row = lax.broadcasted_iota(jnp.int32, (ROWS, ROWS), 0)
     lane = lax.broadcasted_iota(jnp.int32, (ROWS, ROWS), 1)
     pick = row == lane
@@ -319,7 +345,7 @@
         return jnp.sum(jnp.where(pick, wide, 0.0), axis=1, keepdims=True)
 
     weight = column(prior[...])
-    inverse = 1.0 / (weight + column(acc[SUM_ROWS : SUM_ROWS + 1, 0:ROWS]))
+    inverse = 1.0 / (weight + column(mass[:, 0:ROWS]))
     copy.wait()
     for c in range(3):
         numer = weight * held[:, c * 128 : (c + 1) * 128].astype(F32) + acc[
@@ -331,8 +357,15 @@
 def per_device(raw, taps, whitening, basis, project, centroids, prior, times, counts):
     windows = ("section", "lane")
     count = SECTIONS * LANES
-    before = lax.ppermute(raw[SEG - BEFORE :], windows, [(i, i + 1) for i in range(count - 1)])
-    after = lax.ppermute(raw[:AFTER], windows, [(i + 1, i) for i in range(count - 1)])
+    head, tail = call(
+        edges_kernel,
+        (jax.ShapeDtypeStruct((AFTER, CH), BF16), jax.ShapeDtypeStruct((BEFORE, CH), BF16)),
+        [VMEM],
+        (VMEM, VMEM),
+        moved=1_000_000,
+    )(raw)
+    before = lax.ppermute(tail, windows, [(i, i + 1) for i in range(count - 1)])
+    after = lax.ppermute(head, windows, [(i + 1, i) for i in range(count - 1)])
     held = inner(raw, taps.reshape(1, TAPS), whitening, basis.T, times)
     feats = features(before, after, raw, whitening, *held, project)
     spikes = lax.all_gather(feats, "group", axis=0, tiled=True)
@@ -350,9 +383,9 @@
         lax.ppermute(part, "lane", [(i, (i + NEAR * (d + 1)) % LANES) for i in range(LANES)])
         for d, part in enumerate(sent)
     ]
-    total = call(far_kernel, wide, [VMEM] * 4, VMEM, moved=300_000)(own, *took)
+    total, sent = call(far_kernel, (wide, small), [VMEM] * 4, (VMEM,) * 2, moved=300_000)(own, *took)
     earlier = [
-        lax.ppermute(total, "section", [(i, i + d) for i in range(SECTIONS - d)])
+        lax.ppermute(sent, "section", [(i, i + d) for i in range(SECTIONS - d)])
         for d in range(1, SECTIONS)
     ]
     return call(

time: 115 us -> 112 us (0.974)
  local copies, waits for them, and re-layouts: 5.81 us -> 4.1 us
    slice x2 -> x0, local copies, waits for them, and re-layouts: 1.71 us -> none  [the longest x1 0.91 us: per_device(): raw[SEG - BEFORE:]]
  transfers between devices with their start and end apart: 8 -> 8, of which waited for: 4 -> 3; matrix products, arithmetic and copies ran while one was open for 1% -> 0% of each run, Pallas kernels for 5% -> 5%
where the time goes in v3:
time: 112 us
  blocking collectives  45.8 us (41%)
  starting transfers between devices  38.5 us (34%)
  Pallas kernels  11.5 us (10%)
  waiting for transfers between devices  11 us (10%)
  local copies, waits for them, and re-layouts  4.1 us (4%)
    all_to_all x1, blocking collectives, per_device(): got = lax.all_to_all(parts, 'lane', 0, 0, axis_index_groups=near)  23.1 us
    ppermute x3, starting transfers between devices, per_device(): lax.ppermute(part, 'lane', [(i, (i + NEAR * (d + 1)) % LANES) for i in ra...  19.6 us
    all_gather x1, blocking collectives, per_device(): spikes = lax.all_gather(feats, 'group', axis=0, tiled=True)  13.7 us
    ppermute x1, starting transfers between devices, per_device(): after = lax.ppermute(head, windows, [(i + 1, i) for i in range(count - 1)])  11.3 us
    all_to_all x1, blocking collectives, per_device(): shares = lax.all_to_all(shares, 'group', 0, 0)  9.04 us
    ppermute x3, waiting for transfers between devices, per_device(): lax.ppermute(part, 'lane', [(i, (i + NEAR * (d + 1)) % LANES) for i in ra...  6.93 us
    ppermute x3, starting transfers between devices, per_device(): lax.ppermute(sent, 'section', [(i, i + d) for i in range(SECTIONS - d)])  5.64 us
    pallas_call x1, Pallas kernels, inner(): call(inner_kernel, (jax.ShapeDtypeStruct((SPK * 8, CH), F32), jax.ShapeDt...  5.23 us
  transfers between devices with their start and end apart: 8, of which 3 were waited for; matrix products, arithmetic and copies ran while one was open for 0% of the time, Pallas kernels for 5%

profile of v3, /device:TPU:8, one launch (start us, length us, event | category | flops | bytes accessed | tf_op | source)
XLA Modules:
  0.0 111.7 jit_solution(10236237354719659612)
XLA Ops:
  0.0 0.0 copy-start
  0.0 1.1 %copy-done = bf16[1024,384]{1,0:T(8,128)(2,1)S(1)} copy-done((bf16[1024,384]{1,0:T(8,128)(2,1)S(1)}, bf16[1024,384]{1,0:T(8,128)(2,1)}, u32[]{:S(2)}) %copy-start) | copy-done | bytes 786456
  1.2 11.3 %collective-permute-start.1 = (bf16[64,384]{1,0:T(8,128)(2,1)S(1)}, bf16[64,384]{1,0:T(8,128)(2,1)S(1)}, u32[]{:S(2)}, u32[]{:S(2)}) collective-permute-start(bf16[64,384]{1,0:T(8,128)(2,1)S(1)} %get-tuple-element.21), channel_id=1, source_target_pairs={{8,0},{16,8},{24,16},{32,24},{40,32},{48,40},{56,48},{64,56},{72,6... | collective-permute-start | bytes 147464 | tf_op jit(solution)/shard_map/ppermute | solution.py:368
  12.4 1.9 %collective-permute-start = (bf16[128,384]{1,0:T(8,128)(2,1)S(1)}, bf16[128,384]{1,0:T(8,128)(2,1)S(1)}, u32[]{:S(2)}, u32[]{:S(2)}) collective-permute-start(bf16[128,384]{1,0:T(8,128)(2,1)S(1)} %get-tuple-element.20), channel_id=1, source_target_pairs={{0,8},{8,16},{16,24},{24,32},{32,40},{40,48},{48,56},{56,64},{64,7... | collective-permute-start | bytes 294920 | tf_op jit(solution)/shard_map/ppermute | solution.py:367
  14.4 0.0 copy-start.3
  14.4 1.0 copy-done.3
  15.3 0.0 copy-start.5
  15.3 0.7 copy-done.5
  16.0 0.0 copy-start.6
  16.0 0.7 copy-done.6
  16.7 0.0 copy-start.7
  16.7 0.7 copy-done.7
  17.3 0.0 copy-start.1
  17.3 5.2 %shard_map.92 = (f32[1024,384]{1,0:T(8,128)S(1)}, bf16[960,384]{1,0:T(8,128)(2,1)S(1)}, bf16[1024,384]{1,0:T(8,128)(2,1)S(1)}, bf16[384,256]{1,0:T(8,128)(2,1)S(1)}) custom-call(bf16[1024,384]{1,0:T(8,128)(2,1)S(1)} %copy-done, f32[1,64]{1,0:T(1,128)S(1)} %bitcast.3, bf16[384,384]{1,0:T(8,128)(2,1)S(1)} %copy-done.3, bf16[6,121]{1,0:T(8,128)(2,1)S(1)} %bitcast.2, ...), custom_call_target="tpu_custom_call" | custom-call | flops 2000000000 | bytes 6000000 | tf_op jit(solution)/shard_map/pallas_call | solution.py:114
  23.2 0.0 collective-permute-done.1.after
  23.2 0.0 collective-permute-done.before
  23.2 0.0 copy-done.1
  23.3 0.0 copy-start.2
  23.3 1.9 %shard_map.93 = bf16[128,384]{1,0:T(8,128)(2,1)S(1)} custom-call(bf16[128,384]{1,0:T(8,128)(2,1)S(1)} %collective-permute-done.before, bf16[64,384]{1,0:T(8,128)(2,1)S(1)} %collective-permute-done.1.after, bf16[1024,384]{1,0:T(8,128)(2,1)S(1)} %copy-done, bf16[384,384]{1,0:T(8,128)(2,1)S(1)} %copy-done.3, f32[1024,384]{1,0:T(8,128)S(1)} %get-tuple-element.22.found, ...), custom_call_target="tpu_custom_call" | custom-call | flops 1000000000 | bytes 6000000 | tf_op jit(solution)/shard_map/pallas_call | solution.py:172
  25.2 13.7 %all_gather.3.spikes = bf16[1024,384]{1,0:T(8,128)(2,1)S(1)} all-gather(bf16[128,384]{1,0:T(8,128)(2,1)S(1)} %shard_map.93), channel_id=1, replica_groups=mesh['section'=4,'lane'=16,'group'=8] {'group'}, dimensions={0}, use_global_device_ids=true | all-gather | bytes 884736 | tf_op jit(solution)/shard_map/all_gather | solution.py:371
  38.9 0.0 copy-done.2
  38.9 2.0 %shard_map.94 = (f32[8,8,128]{2,1,0:T(8,128)S(1)}, bf16[1024,1024]{1,0:T(8,128)(2,1)S(1)}, f32[8,128]{1,0:T(8,128)S(1)}) custom-call(bf16[1024,384]{1,0:T(8,128)(2,1)S(1)} %all_gather.3.spikes, bf16[1,1024,384]{2,1,0:T(8,128)(2,1)S(1)} %copy-done.2, s32[1,1]{1,0:T(1,128)S(6)} %copy.10.counts), custom_call_target="tpu_custom_call" | custom-call | flops 1000000000 | bytes 4000000 | tf_op jit(solution)/shard_map/pallas_call | solution.py:218
  40.9 9.0 %all_to_all.10.shares = f32[8,8,128]{2,1,0:T(8,128)S(1)} all-to-all(f32[8,8,128]{2,1,0:T(8,128)S(1)} %get-tuple-element.26), channel_id=1, replica_groups=mesh['section'=4,'lane'=16,'group'=8] {'group'}, dimensions={0} | all-to-all | bytes 65536 | tf_op jit(solution)/shard_map/all_to_all | solution.py:373
  49.9 1.3 %shard_map.95 = bf16[4,784,128]{2,1,0:T(8,128)(2,1)S(1)} custom-call(f32[8,8,128]{2,1,0:T(8,128)S(1)} %all_to_all.10.shares, bf16[1024,1024]{1,0:T(8,128)(2,1)S(1)} %get-tuple-element.27.weights, f32[8,128]{1,0:T(8,128)S(1)} %get-tuple-element.28.tops, bf16[1024,384]{1,0:T(8,128)(2,1)S(1)} %all_gather.3.spikes), custom_call_target="tpu_custom_call" | custom-call | flops 1000000000 | bytes 4000000 | tf_op jit(solution)/shard_map/pallas_call | solution.py:285
  51.2 0.0 copy-start.4
  51.2 23.1 %all_to_all.11.got = bf16[4,784,128]{2,1,0:T(8,128)(2,1)S(1)} all-to-all(bf16[4,784,128]{2,1,0:T(8,128)(2,1)S(1)} %shard_map.95), channel_id=1, replica_groups={{0,8,16,24},{32,40,48,56},{64,72,80,88},{96,104,112,120},{1,9,17,25},{3..., dimensions={0} | all-to-all | bytes 1605632 | tf_op jit(solution)/shard_map/all_to_all | solution.py:376
  74.3 0.1 shard_map.96
  74.4 6.0 %collective-permute-start.2 = (bf16[208,128]{1,0:T(8,128)(2,1)S(1)}, bf16[208,128]{1,0:T(8,128)(2,1)S(1)}, u32[]{:S(2)}, u32[]{:S(2)}) collective-permute-start(bf16[208,128]{1,0:T(8,128)(2,1)S(1)} %get-tuple-element.30), channel_id=1, source_target_pairs={{0,32},{8,40},{16,48},{24,56},{32,64},{40,72},{48,80},{56,88},{64,... | collective-permute-start | bytes 159752 | tf_op jit(solution)/shard_map/ppermute | solution.py:383
  80.3 9.2 %collective-permute-start.3 = (bf16[208,128]{1,0:T(8,128)(2,1)S(1)}, bf16[208,128]{1,0:T(8,128)(2,1)S(1)}, u32[]{:S(2)}, u32[]{:S(2)}) collective-permute-start(bf16[208,128]{1,0:T(8,128)(2,1)S(1)} %get-tuple-element.31), channel_id=1, source_target_pairs={{0,64},{8,72},{16,80},{24,88},{32,96},{40,104},{48,112},{56,120},{... | collective-permute-start | bytes 159752 | tf_op jit(solution)/shard_map/ppermute | solution.py:383
  89.5 4.5 %collective-permute-start.4 = (bf16[208,128]{1,0:T(8,128)(2,1)S(1)}, bf16[208,128]{1,0:T(8,128)(2,1)S(1)}, u32[]{:S(2)}, u32[]{:S(2)}) collective-permute-start(bf16[208,128]{1,0:T(8,128)(2,1)S(1)} %get-tuple-element.32), channel_id=1, source_target_pairs={{0,96},{8,104},{16,112},{24,120},{32,0},{40,8},{48,16},{56,24},{64... | collective-permute-start | bytes 159752 | tf_op jit(solution)/shard_map/ppermute | solution.py:383
  94.0 0.0 collective-permute-done.2.one
  94.0 1.3 %collective-permute-done.3.two = bf16[208,128]{1,0:T(8,128)(2,1)S(1)} collective-permute-done((bf16[208,128]{1,0:T(8,128)(2,1)S(1)}, bf16[208,128]{1,0:T(8,128)(2,1)S(1)}, u32[]{:S(2)}, u32[]{:S(2)}) %collective-permute-start.3) | collective-permute-done | bytes 53280 | tf_op jit(solution)/shard_map/ppermute | solution.py:383
  95.4 5.6 %collective-permute-done.4.three = bf16[208,128]{1,0:T(8,128)(2,1)S(1)} collective-permute-done((bf16[208,128]{1,0:T(8,128)(2,1)S(1)}, bf16[208,128]{1,0:T(8,128)(2,1)S(1)}, u32[]{:S(2)}, u32[]{:S(2)}) %collective-permute-start.4) | collective-permute-done | bytes 53280 | tf_op jit(solution)/shard_map/ppermute | solution.py:383
  101.0 0.1 shard_map.97
  101.1 0.7 collective-permute-start.7
  101.7 3.1 %collective-permute-start.6 = (bf16[208,128]{1,0:T(8,128)(2,1)S(1)}, bf16[208,128]{1,0:T(8,128)(2,1)S(1)}, u32[]{:S(2)}, u32[]{:S(2)}) collective-permute-start(bf16[208,128]{1,0:T(8,128)(2,1)S(1)} %get-tuple-element.34), channel_id=1, source_target_pairs={{0,256},{128,384},{1,257},{129,385},{2,258},{130,386},{3,259},{131... | collective-permute-start | bytes 159752 | tf_op jit(solution)/shard_map/ppermute | solution.py:388
  104.8 1.9 %collective-permute-start.5 = (bf16[208,128]{1,0:T(8,128)(2,1)S(1)}, bf16[208,128]{1,0:T(8,128)(2,1)S(1)}, u32[]{:S(2)}, u32[]{:S(2)}) collective-permute-start(bf16[208,128]{1,0:T(8,128)(2,1)S(1)} %get-tuple-element.34), channel_id=1, source_target_pairs={{0,128},{128,256},{256,384},{1,129},{129,257},{257,385},{2,130},{1... | collective-permute-start | bytes 159752 | tf_op jit(solution)/shard_map/ppermute | solution.py:388
  106.7 0.0 collective-permute-done.7.three
  106.7 0.0 collective-permute-done.6.two
  106.7 4.1 %collective-permute-done.5.one = bf16[208,128]{1,0:T(8,128)(2,1)S(1)} collective-permute-done((bf16[208,128]{1,0:T(8,128)(2,1)S(1)}, bf16[208,128]{1,0:T(8,128)(2,1)S(1)}, u32[]{:S(2)}, u32[]{:S(2)}) %collective-permute-start.5) | collective-permute-done | bytes 53280 | tf_op jit(solution)/shard_map/ppermute | solution.py:388
  110.8 0.0 copy-done.4
  110.8 0.9 shard_map.98
  (1 shorter events, 0.0 us)
Async XLA Ops:
  0.0 1.1 %copy-start = (bf16[1024,384]{1,0:T(8,128)(2,1)S(1)}, bf16[1024,384]{1,0:T(8,128)(2,1)}, u32[]{:S(2)}) copy-start(bf16[1024,384]{1,0:T(8,128)(2,1)} %raw.5) | copy-start | bytes 2359300
  1.2 22.1 %collective-permute-start.1 = (bf16[64,384]{1,0:T(8,128)(2,1)S(1)}, bf16[64,384]{1,0:T(8,128)(2,1)S(1)}, u32[]{:S(2)}, u32[]{:S(2)}) collective-permute-start(bf16[64,384]{1,0:T(8,128)(2,1)S(1)} %get-tuple-element.21), channel_id=1, source_target_pairs={{8,0},{16,8},{24,16},{32,24},{40,32},{48,40},{56,48},{64,56},{72,6... | collective-permute-start | bytes 147464 | tf_op jit(solution)/shard_map/ppermute | solution.py:368
  12.4 10.8 %collective-permute-start = (bf16[128,384]{1,0:T(8,128)(2,1)S(1)}, bf16[128,384]{1,0:T(8,128)(2,1)S(1)}, u32[]{:S(2)}, u32[]{:S(2)}) collective-permute-start(bf16[128,384]{1,0:T(8,128)(2,1)S(1)} %get-tuple-element.20), channel_id=1, source_target_pairs={{0,8},{8,16},{16,24},{24,32},{32,40},{40,48},{48,56},{56,64},{64,7... | collective-permute-start | bytes 294920 | tf_op jit(solution)/shard_map/ppermute | solution.py:367
  14.4 1.0 copy-start.3
  15.3 0.7 copy-start.5
  16.0 0.7 copy-start.6
  16.7 0.7 copy-start.7
  17.3 5.9 %copy-start.1 = (bf16[2304,384]{1,0:T(8,128)(2,1)S(1)}, bf16[2304,384]{1,0:T(8,128)(2,1)}, u32[]{:S(2)}) copy-start(bf16[2304,384]{1,0:T(8,128)(2,1)} %project.1) | copy-start | bytes 5308420
  23.3 15.6 %copy-start.2 = (bf16[1,1024,384]{2,1,0:T(8,128)(2,1)S(1)}, bf16[1,1024,384]{2,1,0:T(8,128)(2,1)}, u32[]{:S(2)}) copy-start(bf16[1,1024,384]{2,1,0:T(8,128)(2,1)} %centers.3) | copy-start | bytes 2359300
  51.2 59.6 %copy-start.4 = (f32[1,64]{1,0:T(1,128)S(1)}, f32[1,64]{1,0:T(1,128)}, u32[]{:S(2)}) copy-start(f32[1,64]{1,0:T(1,128)} %prior.1) | copy-start | bytes 772
  74.4 19.7 %collective-permute-start.2 = (bf16[208,128]{1,0:T(8,128)(2,1)S(1)}, bf16[208,128]{1,0:T(8,128)(2,1)S(1)}, u32[]{:S(2)}, u32[]{:S(2)}) collective-permute-start(bf16[208,128]{1,0:T(8,128)(2,1)S(1)} %get-tuple-element.30), channel_id=1, source_target_pairs={{0,32},{8,40},{16,48},{24,56},{32,64},{40,72},{48,80},{56,88},{64,... | collective-permute-start | bytes 159752 | tf_op jit(solution)/shard_map/ppermute | solution.py:383
  80.3 15.0 %collective-permute-start.3 = (bf16[208,128]{1,0:T(8,128)(2,1)S(1)}, bf16[208,128]{1,0:T(8,128)(2,1)S(1)}, u32[]{:S(2)}, u32[]{:S(2)}) collective-permute-start(bf16[208,128]{1,0:T(8,128)(2,1)S(1)} %get-tuple-element.31), channel_id=1, source_target_pairs={{0,64},{8,72},{16,80},{24,88},{32,96},{40,104},{48,112},{56,120},{... | collective-permute-start | bytes 159752 | tf_op jit(solution)/shard_map/ppermute | solution.py:383
  89.5 11.4 %collective-permute-start.4 = (bf16[208,128]{1,0:T(8,128)(2,1)S(1)}, bf16[208,128]{1,0:T(8,128)(2,1)S(1)}, u32[]{:S(2)}, u32[]{:S(2)}) collective-permute-start(bf16[208,128]{1,0:T(8,128)(2,1)S(1)} %get-tuple-element.32), channel_id=1, source_target_pairs={{0,96},{8,104},{16,112},{24,120},{32,0},{40,8},{48,16},{56,24},{64... | collective-permute-start | bytes 159752 | tf_op jit(solution)/shard_map/ppermute | solution.py:383
  101.1 5.7 %collective-permute-start.7 = (bf16[208,128]{1,0:T(8,128)(2,1)S(1)}, bf16[208,128]{1,0:T(8,128)(2,1)S(1)}, u32[]{:S(2)}, u32[]{:S(2)}) collective-permute-start(bf16[208,128]{1,0:T(8,128)(2,1)S(1)} %get-tuple-element.34), channel_id=1, source_target_pairs={{0,384},{1,385},{2,386},{3,387},{4,388},{5,389},{6,390},{7,391},{8... | collective-permute-start | bytes 159752 | tf_op jit(solution)/shard_map/ppermute | solution.py:388
  101.7 5.0 %collective-permute-start.6 = (bf16[208,128]{1,0:T(8,128)(2,1)S(1)}, bf16[208,128]{1,0:T(8,128)(2,1)S(1)}, u32[]{:S(2)}, u32[]{:S(2)}) collective-permute-start(bf16[208,128]{1,0:T(8,128)(2,1)S(1)} %get-tuple-element.34), channel_id=1, source_target_pairs={{0,256},{128,384},{1,257},{129,385},{2,258},{130,386},{3,259},{131... | collective-permute-start | bytes 159752 | tf_op jit(solution)/shard_map/ppermute | solution.py:388
  104.8 6.0 %collective-permute-start.5 = (bf16[208,128]{1,0:T(8,128)(2,1)S(1)}, bf16[208,128]{1,0:T(8,128)(2,1)S(1)}, u32[]{:S(2)}, u32[]{:S(2)}) collective-permute-start(bf16[208,128]{1,0:T(8,128)(2,1)S(1)} %get-tuple-element.34), channel_id=1, source_target_pairs={{0,128},{128,256},{256,384},{1,129},{129,257},{257,385},{2,130},{1... | collective-permute-start | bytes 159752 | tf_op jit(solution)/shard_map/ppermute | solution.py:388

commit v4 on v3

--- a/solution.py
+++ b/solution.py
@@ -90,7 +90,7 @@
         rows[pl.ds(at, 8), pl.ds(start, 256)] = pltpu.roll(shape, u & 127, 1)
         return carry
 
-    lax.fori_loop(0, SPK, put, 0, unroll=8)
+    lax.fori_loop(0, SPK, put, 0, unroll=128)
 
     for b in range(5):
         both = jnp.dot(

time: 112 us -> 111 us (level)
  Pallas kernels: 11.5 us -> 10.2 us
    pallas_call x1, Pallas kernels: 5.23 us -> 3.96 us  [inner(): call(inner_kernel, (jax.ShapeDtypeStruct((SPK * 8, CH), F32), jax.ShapeDt...]
  transfers between devices with their start and end apart: 8 -> 8, of which waited for: 3 -> 3; matrix products, arithmetic and copies ran while one was open for 0% -> 0% of each run, Pallas kernels for 5% -> 4%
where the time goes in v4:
time: 111 us; the launch traced here: 110 us
  blocking collectives  45.8 us (41%)
  starting transfers between devices  38.5 us (35%)
  waiting for transfers between devices  11 us (10%)
  Pallas kernels  10.2 us (9%)
  local copies, waits for them, and re-layouts  4.1 us (4%)
    all_to_all x1, blocking collectives, per_device(): got = lax.all_to_all(parts, 'lane', 0, 0, axis_index_groups=near)  23.1 us
    ppermute x3, starting transfers between devices, per_device(): lax.ppermute(part, 'lane', [(i, (i + NEAR * (d + 1)) % LANES) for i in ra...  19.7 us
    all_gather x1, blocking collectives, per_device(): spikes = lax.all_gather(feats, 'group', axis=0, tiled=True)  13.7 us
    ppermute x1, starting transfers between devices, per_device(): after = lax.ppermute(head, windows, [(i + 1, i) for i in range(count - 1)])  11.3 us
    all_to_all x1, blocking collectives, per_device(): shares = lax.all_to_all(shares, 'group', 0, 0)  9 us
    ppermute x3, waiting for transfers between devices, per_device(): lax.ppermute(part, 'lane', [(i, (i + NEAR * (d + 1)) % LANES) for i in ra...  6.87 us
    ppermute x3, starting transfers between devices, per_device(): lax.ppermute(sent, 'section', [(i, i + d) for i in range(SECTIONS - d)])  5.61 us
    unnamed x16, local copies, waits for them, and re-layouts  4.1 us
  transfers between devices with their start and end apart: 8, of which 3 were waited for; matrix products, arithmetic and copies ran while one was open for 0% of the time, Pallas kernels for 4%

profile of v4, /device:TPU:8, one launch (start us, length us, event | category | flops | bytes accessed | tf_op | source)
XLA Modules:
  0.0 110.4 jit_solution(3235949146680078549)
XLA Ops:
  0.0 0.0 copy-start
  0.0 1.1 %copy-done = bf16[1024,384]{1,0:T(8,128)(2,1)S(1)} copy-done((bf16[1024,384]{1,0:T(8,128)(2,1)S(1)}, bf16[1024,384]{1,0:T(8,128)(2,1)}, u32[]{:S(2)}) %copy-start) | copy-done | bytes 786456
  1.2 11.3 %collective-permute-start.1 = (bf16[64,384]{1,0:T(8,128)(2,1)S(1)}, bf16[64,384]{1,0:T(8,128)(2,1)S(1)}, u32[]{:S(2)}, u32[]{:S(2)}) collective-permute-start(bf16[64,384]{1,0:T(8,128)(2,1)S(1)} %get-tuple-element.21), channel_id=1, source_target_pairs={{8,0},{16,8},{24,16},{32,24},{40,32},{48,40},{56,48},{64,56},{72,6... | collective-permute-start | bytes 147464 | tf_op jit(solution)/shard_map/ppermute | solution.py:368
  12.4 1.9 %collective-permute-start = (bf16[128,384]{1,0:T(8,128)(2,1)S(1)}, bf16[128,384]{1,0:T(8,128)(2,1)S(1)}, u32[]{:S(2)}, u32[]{:S(2)}) collective-permute-start(bf16[128,384]{1,0:T(8,128)(2,1)S(1)} %get-tuple-element.20), channel_id=1, source_target_pairs={{0,8},{8,16},{16,24},{24,32},{32,40},{40,48},{48,56},{56,64},{64,7... | collective-permute-start | bytes 294920 | tf_op jit(solution)/shard_map/ppermute | solution.py:367
  14.4 0.0 copy-start.3
  14.4 1.0 copy-done.3
  15.3 0.0 copy-start.5
  15.3 0.7 copy-done.5
  16.0 0.0 copy-start.6
  16.0 0.7 copy-done.6
  16.7 0.0 copy-start.7
  16.7 0.7 copy-done.7
  17.3 0.0 copy-start.1
  17.3 4.0 %shard_map.92 = (f32[1024,384]{1,0:T(8,128)S(1)}, bf16[960,384]{1,0:T(8,128)(2,1)S(1)}, bf16[1024,384]{1,0:T(8,128)(2,1)S(1)}, bf16[384,256]{1,0:T(8,128)(2,1)S(1)}) custom-call(bf16[1024,384]{1,0:T(8,128)(2,1)S(1)} %copy-done, f32[1,64]{1,0:T(1,128)S(1)} %bitcast.3, bf16[384,384]{1,0:T(8,128)(2,1)S(1)} %copy-done.3, bf16[6,121]{1,0:T(8,128)(2,1)S(1)} %bitcast.2, ...), custom_call_target="tpu_custom_call" | custom-call | flops 2000000000 | bytes 6000000 | tf_op jit(solution)/shard_map/pallas_call | solution.py:114
  22.0 0.0 collective-permute-done.1.after
  22.0 0.0 collective-permute-done.before
  22.0 0.0 copy-done.1
  22.0 0.0 copy-start.2
  22.0 1.9 %shard_map.93 = bf16[128,384]{1,0:T(8,128)(2,1)S(1)} custom-call(bf16[128,384]{1,0:T(8,128)(2,1)S(1)} %collective-permute-done.before, bf16[64,384]{1,0:T(8,128)(2,1)S(1)} %collective-permute-done.1.after, bf16[1024,384]{1,0:T(8,128)(2,1)S(1)} %copy-done, bf16[384,384]{1,0:T(8,128)(2,1)S(1)} %copy-done.3, f32[1024,384]{1,0:T(8,128)S(1)} %get-tuple-element.22.found, ...), custom_call_target="tpu_custom_call" | custom-call | flops 1000000000 | bytes 6000000 | tf_op jit(solution)/shard_map/pallas_call | solution.py:172
  23.9 13.7 %all_gather.3.spikes = bf16[1024,384]{1,0:T(8,128)(2,1)S(1)} all-gather(bf16[128,384]{1,0:T(8,128)(2,1)S(1)} %shard_map.93), channel_id=1, replica_groups=mesh['section'=4,'lane'=16,'group'=8] {'group'}, dimensions={0}, use_global_device_ids=true | all-gather | bytes 884736 | tf_op jit(solution)/shard_map/all_gather | solution.py:371
  37.7 0.0 copy-done.2
  37.7 2.0 %shard_map.94 = (f32[8,8,128]{2,1,0:T(8,128)S(1)}, bf16[1024,1024]{1,0:T(8,128)(2,1)S(1)}, f32[8,128]{1,0:T(8,128)S(1)}) custom-call(bf16[1024,384]{1,0:T(8,128)(2,1)S(1)} %all_gather.3.spikes, bf16[1,1024,384]{2,1,0:T(8,128)(2,1)S(1)} %copy-done.2, s32[1,1]{1,0:T(1,128)S(6)} %copy.10.counts), custom_call_target="tpu_custom_call" | custom-call | flops 1000000000 | bytes 4000000 | tf_op jit(solution)/shard_map/pallas_call | solution.py:218
  39.6 9.0 %all_to_all.10.shares = f32[8,8,128]{2,1,0:T(8,128)S(1)} all-to-all(f32[8,8,128]{2,1,0:T(8,128)S(1)} %get-tuple-element.26), channel_id=1, replica_groups=mesh['section'=4,'lane'=16,'group'=8] {'group'}, dimensions={0} | all-to-all | bytes 65536 | tf_op jit(solution)/shard_map/all_to_all | solution.py:373
  48.6 1.3 %shard_map.95 = bf16[4,784,128]{2,1,0:T(8,128)(2,1)S(1)} custom-call(f32[8,8,128]{2,1,0:T(8,128)S(1)} %all_to_all.10.shares, bf16[1024,1024]{1,0:T(8,128)(2,1)S(1)} %get-tuple-element.27.weights, f32[8,128]{1,0:T(8,128)S(1)} %get-tuple-element.28.tops, bf16[1024,384]{1,0:T(8,128)(2,1)S(1)} %all_gather.3.spikes), custom_call_target="tpu_custom_call" | custom-call | flops 1000000000 | bytes 4000000 | tf_op jit(solution)/shard_map/pallas_call | solution.py:285
  49.9 0.0 copy-start.4
  49.9 23.1 %all_to_all.11.got = bf16[4,784,128]{2,1,0:T(8,128)(2,1)S(1)} all-to-all(bf16[4,784,128]{2,1,0:T(8,128)(2,1)S(1)} %shard_map.95), channel_id=1, replica_groups={{0,8,16,24},{32,40,48,56},{64,72,80,88},{96,104,112,120},{1,9,17,25},{3..., dimensions={0} | all-to-all | bytes 1605632 | tf_op jit(solution)/shard_map/all_to_all | solution.py:376
  73.0 0.1 shard_map.96
  73.1 6.0 %collective-permute-start.2 = (bf16[208,128]{1,0:T(8,128)(2,1)S(1)}, bf16[208,128]{1,0:T(8,128)(2,1)S(1)}, u32[]{:S(2)}, u32[]{:S(2)}) collective-permute-start(bf16[208,128]{1,0:T(8,128)(2,1)S(1)} %get-tuple-element.30), channel_id=1, source_target_pairs={{0,32},{8,40},{16,48},{24,56},{32,64},{40,72},{48,80},{56,88},{64,... | collective-permute-start | bytes 159752 | tf_op jit(solution)/shard_map/ppermute | solution.py:383
  79.1 9.1 %collective-permute-start.3 = (bf16[208,128]{1,0:T(8,128)(2,1)S(1)}, bf16[208,128]{1,0:T(8,128)(2,1)S(1)}, u32[]{:S(2)}, u32[]{:S(2)}) collective-permute-start(bf16[208,128]{1,0:T(8,128)(2,1)S(1)} %get-tuple-element.31), channel_id=1, source_target_pairs={{0,64},{8,72},{16,80},{24,88},{32,96},{40,104},{48,112},{56,120},{... | collective-permute-start | bytes 159752 | tf_op jit(solution)/shard_map/ppermute | solution.py:383
  88.2 4.6 %collective-permute-start.4 = (bf16[208,128]{1,0:T(8,128)(2,1)S(1)}, bf16[208,128]{1,0:T(8,128)(2,1)S(1)}, u32[]{:S(2)}, u32[]{:S(2)}) collective-permute-start(bf16[208,128]{1,0:T(8,128)(2,1)S(1)} %get-tuple-element.32), channel_id=1, source_target_pairs={{0,96},{8,104},{16,112},{24,120},{32,0},{40,8},{48,16},{56,24},{64... | collective-permute-start | bytes 159752 | tf_op jit(solution)/shard_map/ppermute | solution.py:383
  92.8 0.0 collective-permute-done.2.one
  92.8 1.3 %collective-permute-done.3.two = bf16[208,128]{1,0:T(8,128)(2,1)S(1)} collective-permute-done((bf16[208,128]{1,0:T(8,128)(2,1)S(1)}, bf16[208,128]{1,0:T(8,128)(2,1)S(1)}, u32[]{:S(2)}, u32[]{:S(2)}) %collective-permute-start.3) | collective-permute-done | bytes 53280 | tf_op jit(solution)/shard_map/ppermute | solution.py:383
  94.1 5.5 %collective-permute-done.4.three = bf16[208,128]{1,0:T(8,128)(2,1)S(1)} collective-permute-done((bf16[208,128]{1,0:T(8,128)(2,1)S(1)}, bf16[208,128]{1,0:T(8,128)(2,1)S(1)}, u32[]{:S(2)}, u32[]{:S(2)}) %collective-permute-start.4) | collective-permute-done | bytes 53280 | tf_op jit(solution)/shard_map/ppermute | solution.py:383
  99.7 0.1 shard_map.97
  99.8 0.7 collective-permute-start.7
  100.4 3.0 %collective-permute-start.6 = (bf16[208,128]{1,0:T(8,128)(2,1)S(1)}, bf16[208,128]{1,0:T(8,128)(2,1)S(1)}, u32[]{:S(2)}, u32[]{:S(2)}) collective-permute-start(bf16[208,128]{1,0:T(8,128)(2,1)S(1)} %get-tuple-element.34), channel_id=1, source_target_pairs={{0,256},{128,384},{1,257},{129,385},{2,258},{130,386},{3,259},{131... | collective-permute-start | bytes 159752 | tf_op jit(solution)/shard_map/ppermute | solution.py:388
  103.5 1.9 %collective-permute-start.5 = (bf16[208,128]{1,0:T(8,128)(2,1)S(1)}, bf16[208,128]{1,0:T(8,128)(2,1)S(1)}, u32[]{:S(2)}, u32[]{:S(2)}) collective-permute-start(bf16[208,128]{1,0:T(8,128)(2,1)S(1)} %get-tuple-element.34), channel_id=1, source_target_pairs={{0,128},{128,256},{256,384},{1,129},{129,257},{257,385},{2,130},{1... | collective-permute-start | bytes 159752 | tf_op jit(solution)/shard_map/ppermute | solution.py:388
  105.4 0.0 collective-permute-done.7.three
  105.4 0.0 collective-permute-done.6.two
  105.4 4.1 %collective-permute-done.5.one = bf16[208,128]{1,0:T(8,128)(2,1)S(1)} collective-permute-done((bf16[208,128]{1,0:T(8,128)(2,1)S(1)}, bf16[208,128]{1,0:T(8,128)(2,1)S(1)}, u32[]{:S(2)}, u32[]{:S(2)}) %collective-permute-start.5) | collective-permute-done | bytes 53280 | tf_op jit(solution)/shard_map/ppermute | solution.py:388
  109.5 0.0 copy-done.4
  109.5 0.9 shard_map.98
  (1 shorter events, 0.0 us)
Async XLA Ops:
  0.0 1.1 %copy-start = (bf16[1024,384]{1,0:T(8,128)(2,1)S(1)}, bf16[1024,384]{1,0:T(8,128)(2,1)}, u32[]{:S(2)}) copy-start(bf16[1024,384]{1,0:T(8,128)(2,1)} %raw.5) | copy-start | bytes 2359300
  1.2 20.8 %collective-permute-start.1 = (bf16[64,384]{1,0:T(8,128)(2,1)S(1)}, bf16[64,384]{1,0:T(8,128)(2,1)S(1)}, u32[]{:S(2)}, u32[]{:S(2)}) collective-permute-start(bf16[64,384]{1,0:T(8,128)(2,1)S(1)} %get-tuple-element.21), channel_id=1, source_target_pairs={{8,0},{16,8},{24,16},{32,24},{40,32},{48,40},{56,48},{64,56},{72,6... | collective-permute-start | bytes 147464 | tf_op jit(solution)/shard_map/ppermute | solution.py:368
  12.4 9.5 %collective-permute-start = (bf16[128,384]{1,0:T(8,128)(2,1)S(1)}, bf16[128,384]{1,0:T(8,128)(2,1)S(1)}, u32[]{:S(2)}, u32[]{:S(2)}) collective-permute-start(bf16[128,384]{1,0:T(8,128)(2,1)S(1)} %get-tuple-element.20), channel_id=1, source_target_pairs={{0,8},{8,16},{16,24},{24,32},{32,40},{40,48},{48,56},{56,64},{64,7... | collective-permute-start | bytes 294920 | tf_op jit(solution)/shard_map/ppermute | solution.py:367
  14.4 1.0 copy-start.3
  15.3 0.7 copy-start.5
  16.0 0.7 copy-start.6
  16.7 0.7 copy-start.7
  17.3 4.6 %copy-start.1 = (bf16[2304,384]{1,0:T(8,128)(2,1)S(1)}, bf16[2304,384]{1,0:T(8,128)(2,1)}, u32[]{:S(2)}) copy-start(bf16[2304,384]{1,0:T(8,128)(2,1)} %project.1) | copy-start | bytes 5308420
  22.0 15.7 %copy-start.2 = (bf16[1,1024,384]{2,1,0:T(8,128)(2,1)S(1)}, bf16[1,1024,384]{2,1,0:T(8,128)(2,1)}, u32[]{:S(2)}) copy-start(bf16[1,1024,384]{2,1,0:T(8,128)(2,1)} %centers.3) | copy-start | bytes 2359300
  49.9 59.6 %copy-start.4 = (f32[1,64]{1,0:T(1,128)S(1)}, f32[1,64]{1,0:T(1,128)}, u32[]{:S(2)}) copy-start(f32[1,64]{1,0:T(1,128)} %prior.1) | copy-start | bytes 772
  73.1 19.7 %collective-permute-start.2 = (bf16[208,128]{1,0:T(8,128)(2,1)S(1)}, bf16[208,128]{1,0:T(8,128)(2,1)S(1)}, u32[]{:S(2)}, u32[]{:S(2)}) collective-permute-start(bf16[208,128]{1,0:T(8,128)(2,1)S(1)} %get-tuple-element.30), channel_id=1, source_target_pairs={{0,32},{8,40},{16,48},{24,56},{32,64},{40,72},{48,80},{56,88},{64,... | collective-permute-start | bytes 159752 | tf_op jit(solution)/shard_map/ppermute | solution.py:383
  79.1 15.0 %collective-permute-start.3 = (bf16[208,128]{1,0:T(8,128)(2,1)S(1)}, bf16[208,128]{1,0:T(8,128)(2,1)S(1)}, u32[]{:S(2)}, u32[]{:S(2)}) collective-permute-start(bf16[208,128]{1,0:T(8,128)(2,1)S(1)} %get-tuple-element.31), channel_id=1, source_target_pairs={{0,64},{8,72},{16,80},{24,88},{32,96},{40,104},{48,112},{56,120},{... | collective-permute-start | bytes 159752 | tf_op jit(solution)/shard_map/ppermute | solution.py:383
  88.2 11.4 %collective-permute-start.4 = (bf16[208,128]{1,0:T(8,128)(2,1)S(1)}, bf16[208,128]{1,0:T(8,128)(2,1)S(1)}, u32[]{:S(2)}, u32[]{:S(2)}) collective-permute-start(bf16[208,128]{1,0:T(8,128)(2,1)S(1)} %get-tuple-element.32), channel_id=1, source_target_pairs={{0,96},{8,104},{16,112},{24,120},{32,0},{40,8},{48,16},{56,24},{64... | collective-permute-start | bytes 159752 | tf_op jit(solution)/shard_map/ppermute | solution.py:383
  99.8 5.6 %collective-permute-start.7 = (bf16[208,128]{1,0:T(8,128)(2,1)S(1)}, bf16[208,128]{1,0:T(8,128)(2,1)S(1)}, u32[]{:S(2)}, u32[]{:S(2)}) collective-permute-start(bf16[208,128]{1,0:T(8,128)(2,1)S(1)} %get-tuple-element.34), channel_id=1, source_target_pairs={{0,384},{1,385},{2,386},{3,387},{4,388},{5,389},{6,390},{7,391},{8... | collective-permute-start | bytes 159752 | tf_op jit(solution)/shard_map/ppermute | solution.py:388
  100.4 5.0 %collective-permute-start.6 = (bf16[208,128]{1,0:T(8,128)(2,1)S(1)}, bf16[208,128]{1,0:T(8,128)(2,1)S(1)}, u32[]{:S(2)}, u32[]{:S(2)}) collective-permute-start(bf16[208,128]{1,0:T(8,128)(2,1)S(1)} %get-tuple-element.34), channel_id=1, source_target_pairs={{0,256},{128,384},{1,257},{129,385},{2,258},{130,386},{3,259},{131... | collective-permute-start | bytes 159752 | tf_op jit(solution)/shard_map/ppermute | solution.py:388
  103.5 6.0 %collective-permute-start.5 = (bf16[208,128]{1,0:T(8,128)(2,1)S(1)}, bf16[208,128]{1,0:T(8,128)(2,1)S(1)}, u32[]{:S(2)}, u32[]{:S(2)}) collective-permute-start(bf16[208,128]{1,0:T(8,128)(2,1)S(1)} %get-tuple-element.34), channel_id=1, source_target_pairs={{0,128},{128,256},{256,384},{1,129},{129,257},{257,385},{2,130},{1... | collective-permute-start | bytes 159752 | tf_op jit(solution)/shard_map/ppermute | solution.py:388

commit v5 on v4

--- a/solution.py
+++ b/solution.py
@@ -65,10 +65,7 @@
     tail[...] = raw[SEG - BEFORE : SEG, :]
 
 
-def inner_kernel(
-    raw, taps, whitening, basis, times, found, middle, place, band,
-    row, snip, rows,
-):
+def place_kernel(taps, basis, times, core, place, band, row, snip, rows):
     row[...] = jnp.zeros_like(row)
     row[0:1, 0:TAPS] = taps[...]
     spread = jnp.broadcast_to(row[0:1, :], (SPAN, SPAN))
@@ -92,6 +89,12 @@
 
     lax.fori_loop(0, SPK, put, 0, unroll=128)
 
+    place[:, 0:HEAD] = rows[:, 0:HEAD].astype(BF16)
+    place[:, HEAD:EDGE] = rows[:, LATE:PLACE].astype(BF16)
+    core[...] = rows[:, HEAD:LATE].astype(BF16)
+
+
+def inner_kernel(raw, whitening, core, band, found, middle):
     for b in range(5):
         both = jnp.dot(
             band[...], raw[b * BLOCK : b * BLOCK + SPAN, :], preferred_element_type=F32
@@ -102,33 +105,41 @@
         ).astype(BF16)
     for c in range(4):
         part = slice(c * 256, (c + 1) * 256)
-        place[part, 0:HEAD] = rows[part, 0:HEAD].astype(BF16)
-        place[part, HEAD:EDGE] = rows[part, LATE:PLACE].astype(BF16)
         found[part, :] = jnp.dot(
-            rows[part, HEAD:LATE].astype(BF16), middle[0 : LATE - HEAD, :],
-            preferred_element_type=F32,
+            core[part, :], middle[0 : LATE - HEAD, :], preferred_element_type=F32
         )
 
 
 def inner(raw, taps, whitening, basis, times):
-    return call(
-        inner_kernel,
+    core, place, band = call(
+        place_kernel,
         (
-            jax.ShapeDtypeStruct((SPK * 8, CH), F32),
-            jax.ShapeDtypeStruct((MIDDLE, CH), BF16),
+            jax.ShapeDtypeStruct((SPK * 8, LATE - HEAD), BF16),
             jax.ShapeDtypeStruct((SPK * 8, EDGE), BF16),
             jax.ShapeDtypeStruct((2 * BLOCK, SPAN), BF16),
         ),
-        [VMEM, VMEM, VMEM, VMEM, SMEM],
-        (VMEM, VMEM, VMEM, VMEM),
+        [VMEM, VMEM, SMEM],
+        (VMEM, VMEM, VMEM),
         [
             pltpu.VMEM((8, SPAN), F32),
             pltpu.VMEM((8, 256), F32),
             pltpu.VMEM((SPK * 8, PLACE), F32),
         ],
+        flops=500_000_000,
+        moved=8_000_000,
+    )(taps, basis, times)
+    found, middle = call(
+        inner_kernel,
+        (
+            jax.ShapeDtypeStruct((SPK * 8, CH), F32),
+            jax.ShapeDtypeStruct((MIDDLE, CH), BF16),
+        ),
+        [VMEM] * 4,
+        (VMEM, VMEM),
         flops=2_000_000_000,
         moved=6_000_000,
-    )(raw, taps, whitening, basis, times)
+    )(raw, whitening, core, band)
+    return found, middle, place, band
 
 
 def features_kernel(

time: 111 us -> 111 us (level)
  the two profiles are of different devices: /device:TPU:8 before, /device:TPU:24 now
where the time goes in v5:
time: 111 us; the launch traced here: 110 us
  blocking collectives  45.8 us (41%)
  starting transfers between devices  36.6 us (33%)
  waiting for transfers between devices  13.4 us (12%)
  Pallas kernels  10.7 us (10%)
  local copies, waits for them, and re-layouts  3.15 us (3%)
    all_to_all x1, blocking collectives, per_device(): got = lax.all_to_all(parts, 'lane', 0, 0, axis_index_groups=near)  23.1 us
    ppermute x3, starting transfers between devices, per_device(): lax.ppermute(part, 'lane', [(i, (i + NEAR * (d + 1)) % LANES) for i in ra...  19.1 us
    all_gather x1, blocking collectives, per_device(): spikes = lax.all_gather(feats, 'group', axis=0, tiled=True)  13.7 us
    ppermute x1, starting transfers between devices, per_device(): after = lax.ppermute(head, windows, [(i + 1, i) for i in range(count - 1)])  9.68 us
    all_to_all x1, blocking collectives, per_device(): shares = lax.all_to_all(shares, 'group', 0, 0)  9 us
    ppermute x3, waiting for transfers between devices, per_device(): lax.ppermute(sent, 'section', [(i, i + d) for i in range(SECTIONS - d)])  8.02 us
    ppermute x3, waiting for transfers between devices, per_device(): lax.ppermute(part, 'lane', [(i, (i + NEAR * (d + 1)) % LANES) for i in ra...  5.35 us
    ppermute x1, starting transfers between devices, per_device(): before = lax.ppermute(tail, windows, [(i, i + 1) for i in range(count - 1)])  3.96 us
  transfers between devices with their start and end apart: 8, of which 5 were waited for; matrix products, arithmetic and copies ran while one was open for 0% of the time, Pallas kernels for 4%

profile of v5, /device:TPU:24, one launch (start us, length us, event | category | flops | bytes accessed | tf_op | source)
XLA Modules:
  0.0 110.4 jit_solution(18338670136767858971)
XLA Ops:
  0.0 0.0 copy-start
  0.0 1.1 %copy-done = bf16[1024,384]{1,0:T(8,128)(2,1)S(1)} copy-done((bf16[1024,384]{1,0:T(8,128)(2,1)S(1)}, bf16[1024,384]{1,0:T(8,128)(2,1)}, u32[]{:S(2)}) %copy-start) | copy-done | bytes 786456
  1.1 0.0 copy-start.1
  1.1 0.0 copy-start.4
  1.2 4.0 %collective-permute-start = (bf16[128,384]{1,0:T(8,128)(2,1)S(1)}, bf16[128,384]{1,0:T(8,128)(2,1)S(1)}, u32[]{:S(2)}, u32[]{:S(2)}) collective-permute-start(bf16[128,384]{1,0:T(8,128)(2,1)S(1)} %get-tuple-element.21), channel_id=1, source_target_pairs={{0,8},{8,16},{16,24},{24,32},{32,40},{40,48},{48,56},{56,64},{64,7... | collective-permute-start | bytes 294920 | tf_op jit(solution)/shard_map/ppermute | solution.py:378
  5.1 9.7 %collective-permute-start.1 = (bf16[64,384]{1,0:T(8,128)(2,1)S(1)}, bf16[64,384]{1,0:T(8,128)(2,1)S(1)}, u32[]{:S(2)}, u32[]{:S(2)}) collective-permute-start(bf16[64,384]{1,0:T(8,128)(2,1)S(1)} %get-tuple-element.22), channel_id=1, source_target_pairs={{8,0},{16,8},{24,16},{32,24},{40,32},{48,40},{56,48},{64,56},{72,6... | collective-permute-start | bytes 147464 | tf_op jit(solution)/shard_map/ppermute | solution.py:379
  14.8 0.0 copy-start.6
  14.8 0.7 copy-done.6
  15.5 0.0 copy-start.7
  15.5 0.7 copy-done.7
  16.1 0.0 copy-start.8
  16.1 0.7 copy-done.8
  16.8 1.9 %shard_map.92 = (bf16[1024,896]{1,0:T(8,128)(2,1)S(1)}, bf16[1024,384]{1,0:T(8,128)(2,1)S(1)}, bf16[384,256]{1,0:T(8,128)(2,1)S(1)}) custom-call(f32[1,64]{1,0:T(1,128)S(1)} %bitcast.3, bf16[6,121]{1,0:T(8,128)(2,1)S(1)} %bitcast.2, s32[1,1,128]{2,1,0:T(1,128)S(1)} %copy-done.8), custom_call_target="tpu_custom_call" | custom-call | flops 500000000 | bytes 8000000 | tf_op jit(solution)/shard_map/pallas_call | solution.py:114
  18.7 0.0 copy-done.1
  18.7 0.0 copy-done.4
  18.7 0.0 copy-start.2
  18.7 2.6 %shard_map.93 = (f32[1024,384]{1,0:T(8,128)S(1)}, bf16[960,384]{1,0:T(8,128)(2,1)S(1)}) custom-call(bf16[1024,384]{1,0:T(8,128)(2,1)S(1)} %copy-done.1, bf16[384,384]{1,0:T(8,128)(2,1)S(1)} %copy-done.4, bf16[1024,896]{1,0:T(8,128)(2,1)S(1)} %get-tuple-element.23.core, bf16[384,256]{1,0:T(8,128)(2,1)S(1)} %get-tuple-element.24.band), custom_call_target="tpu_custom_call" | custom-call | flops 2000000000 | bytes 6000000 | tf_op jit(solution)/shard_map/pallas_call | solution.py:131
  22.0 0.0 collective-permute-done.1.after
  22.0 0.0 collective-permute-done.before
  22.0 0.0 copy-done.2
  22.0 0.0 copy-start.3
  22.0 1.9 %shard_map.94 = bf16[128,384]{1,0:T(8,128)(2,1)S(1)} custom-call(bf16[128,384]{1,0:T(8,128)(2,1)S(1)} %collective-permute-done.before, bf16[64,384]{1,0:T(8,128)(2,1)S(1)} %collective-permute-done.1.after, bf16[1024,384]{1,0:T(8,128)(2,1)S(1)} %copy-done.1, bf16[384,384]{1,0:T(8,128)(2,1)S(1)} %copy-done.4, f32[1024,384]{1,0:T(8,128)S(1)} %get-tuple-element.25.found, ...), custom_call_target="tpu_custom_call" | custom-call | flops 1000000000 | bytes 6000000 | tf_op jit(solution)/shard_map/pallas_call | solution.py:183
  23.9 13.7 %all_gather.3.spikes = bf16[1024,384]{1,0:T(8,128)(2,1)S(1)} all-gather(bf16[128,384]{1,0:T(8,128)(2,1)S(1)} %shard_map.94), channel_id=1, replica_groups=mesh['section'=4,'lane'=16,'group'=8] {'group'}, dimensions={0}, use_global_device_ids=true | all-gather | bytes 884736 | tf_op jit(solution)/shard_map/all_gather | solution.py:382
  37.6 0.0 copy-done.3
  37.7 2.0 %shard_map.95 = (f32[8,8,128]{2,1,0:T(8,128)S(1)}, bf16[1024,1024]{1,0:T(8,128)(2,1)S(1)}, f32[8,128]{1,0:T(8,128)S(1)}) custom-call(bf16[1024,384]{1,0:T(8,128)(2,1)S(1)} %all_gather.3.spikes, bf16[1,1024,384]{2,1,0:T(8,128)(2,1)S(1)} %copy-done.3, s32[1,1]{1,0:T(1,128)S(6)} %copy.10.counts), custom_call_target="tpu_custom_call" | custom-call | flops 1000000000 | bytes 4000000 | tf_op jit(solution)/shard_map/pallas_call | solution.py:229
  39.6 9.0 %all_to_all.10.shares = f32[8,8,128]{2,1,0:T(8,128)S(1)} all-to-all(f32[8,8,128]{2,1,0:T(8,128)S(1)} %get-tuple-element.28), channel_id=1, replica_groups=mesh['section'=4,'lane'=16,'group'=8] {'group'}, dimensions={0} | all-to-all | bytes 65536 | tf_op jit(solution)/shard_map/all_to_all | solution.py:384
  48.6 1.3 %shard_map.96 = bf16[4,784,128]{2,1,0:T(8,128)(2,1)S(1)} custom-call(f32[8,8,128]{2,1,0:T(8,128)S(1)} %all_to_all.10.shares, bf16[1024,1024]{1,0:T(8,128)(2,1)S(1)} %get-tuple-element.29.weights, f32[8,128]{1,0:T(8,128)S(1)} %get-tuple-element.30.tops, bf16[1024,384]{1,0:T(8,128)(2,1)S(1)} %all_gather.3.spikes), custom_call_target="tpu_custom_call" | custom-call | flops 1000000000 | bytes 4000000 | tf_op jit(solution)/shard_map/pallas_call | solution.py:296
  49.9 0.0 copy-start.5
  49.9 23.1 %all_to_all.11.got = bf16[4,784,128]{2,1,0:T(8,128)(2,1)S(1)} all-to-all(bf16[4,784,128]{2,1,0:T(8,128)(2,1)S(1)} %shard_map.96), channel_id=1, replica_groups={{0,8,16,24},{32,40,48,56},{64,72,80,88},{96,104,112,120},{1,9,17,25},{3..., dimensions={0} | all-to-all | bytes 1605632 | tf_op jit(solution)/shard_map/all_to_all | solution.py:387
  73.0 0.1 shard_map.97
  73.1 5.6 %collective-permute-start.2 = (bf16[208,128]{1,0:T(8,128)(2,1)S(1)}, bf16[208,128]{1,0:T(8,128)(2,1)S(1)}, u32[]{:S(2)}, u32[]{:S(2)}) collective-permute-start(bf16[208,128]{1,0:T(8,128)(2,1)S(1)} %get-tuple-element.32), channel_id=1, source_target_pairs={{0,32},{8,40},{16,48},{24,56},{32,64},{40,72},{48,80},{56,88},{64,... | collective-permute-start | bytes 159752 | tf_op jit(solution)/shard_map/ppermute | solution.py:394
  78.7 8.0 %collective-permute-start.3 = (bf16[208,128]{1,0:T(8,128)(2,1)S(1)}, bf16[208,128]{1,0:T(8,128)(2,1)S(1)}, u32[]{:S(2)}, u32[]{:S(2)}) collective-permute-start(bf16[208,128]{1,0:T(8,128)(2,1)S(1)} %get-tuple-element.33), channel_id=1, source_target_pairs={{0,64},{8,72},{16,80},{24,88},{32,96},{40,104},{48,112},{56,120},{... | collective-permute-start | bytes 159752 | tf_op jit(solution)/shard_map/ppermute | solution.py:394
  86.7 5.5 %collective-permute-start.4 = (bf16[208,128]{1,0:T(8,128)(2,1)S(1)}, bf16[208,128]{1,0:T(8,128)(2,1)S(1)}, u32[]{:S(2)}, u32[]{:S(2)}) collective-permute-start(bf16[208,128]{1,0:T(8,128)(2,1)S(1)} %get-tuple-element.34), channel_id=1, source_target_pairs={{0,96},{8,104},{16,112},{24,120},{32,0},{40,8},{48,16},{56,24},{64... | collective-permute-start | bytes 159752 | tf_op jit(solution)/shard_map/ppermute | solution.py:394
  92.2 0.0 collective-permute-done.2.one
  92.2 1.9 %collective-permute-done.3.two = bf16[208,128]{1,0:T(8,128)(2,1)S(1)} collective-permute-done((bf16[208,128]{1,0:T(8,128)(2,1)S(1)}, bf16[208,128]{1,0:T(8,128)(2,1)S(1)}, u32[]{:S(2)}, u32[]{:S(2)}) %collective-permute-start.3) | collective-permute-done | bytes 53280 | tf_op jit(solution)/shard_map/ppermute | solution.py:394
  94.1 3.4 %collective-permute-done.4.three = bf16[208,128]{1,0:T(8,128)(2,1)S(1)} collective-permute-done((bf16[208,128]{1,0:T(8,128)(2,1)S(1)}, bf16[208,128]{1,0:T(8,128)(2,1)S(1)}, u32[]{:S(2)}, u32[]{:S(2)}) %collective-permute-start.4) | collective-permute-done | bytes 53280 | tf_op jit(solution)/shard_map/ppermute | solution.py:394
  97.6 0.1 shard_map.98
  97.6 1.3 %collective-permute-start.5 = (bf16[208,128]{1,0:T(8,128)(2,1)S(1)}, bf16[208,128]{1,0:T(8,128)(2,1)S(1)}, u32[]{:S(2)}, u32[]{:S(2)}) collective-permute-start(bf16[208,128]{1,0:T(8,128)(2,1)S(1)} %get-tuple-element.36), channel_id=1, source_target_pairs={{0,128},{128,256},{256,384},{1,129},{129,257},{257,385},{2,130},{1... | collective-permute-start | bytes 159752 | tf_op jit(solution)/shard_map/ppermute | solution.py:399
  98.9 1.3 %collective-permute-start.6 = (bf16[208,128]{1,0:T(8,128)(2,1)S(1)}, bf16[208,128]{1,0:T(8,128)(2,1)S(1)}, u32[]{:S(2)}, u32[]{:S(2)}) collective-permute-start(bf16[208,128]{1,0:T(8,128)(2,1)S(1)} %get-tuple-element.36), channel_id=1, source_target_pairs={{0,256},{128,384},{1,257},{129,385},{2,258},{130,386},{3,259},{131... | collective-permute-start | bytes 159752 | tf_op jit(solution)/shard_map/ppermute | solution.py:399
  100.2 1.3 %collective-permute-start.7 = (bf16[208,128]{1,0:T(8,128)(2,1)S(1)}, bf16[208,128]{1,0:T(8,128)(2,1)S(1)}, u32[]{:S(2)}, u32[]{:S(2)}) collective-permute-start(bf16[208,128]{1,0:T(8,128)(2,1)S(1)} %get-tuple-element.36), channel_id=1, source_target_pairs={{0,384},{1,385},{2,386},{3,387},{4,388},{5,389},{6,390},{7,391},{8... | collective-permute-start | bytes 159752 | tf_op jit(solution)/shard_map/ppermute | solution.py:399
  101.5 2.1 %collective-permute-done.5.one = bf16[208,128]{1,0:T(8,128)(2,1)S(1)} collective-permute-done((bf16[208,128]{1,0:T(8,128)(2,1)S(1)}, bf16[208,128]{1,0:T(8,128)(2,1)S(1)}, u32[]{:S(2)}, u32[]{:S(2)}) %collective-permute-start.5) | collective-permute-done | bytes 53280 | tf_op jit(solution)/shard_map/ppermute | solution.py:399
  103.7 2.9 %collective-permute-done.6.two = bf16[208,128]{1,0:T(8,128)(2,1)S(1)} collective-permute-done((bf16[208,128]{1,0:T(8,128)(2,1)S(1)}, bf16[208,128]{1,0:T(8,128)(2,1)S(1)}, u32[]{:S(2)}, u32[]{:S(2)}) %collective-permute-start.6) | collective-permute-done | bytes 53280 | tf_op jit(solution)/shard_map/ppermute | solution.py:399
  106.6 3.0 %collective-permute-done.7.three = bf16[208,128]{1,0:T(8,128)(2,1)S(1)} collective-permute-done((bf16[208,128]{1,0:T(8,128)(2,1)S(1)}, bf16[208,128]{1,0:T(8,128)(2,1)S(1)}, u32[]{:S(2)}, u32[]{:S(2)}) %collective-permute-start.7) | collective-permute-done | bytes 53280 | tf_op jit(solution)/shard_map/ppermute | solution.py:399
  109.5 0.0 copy-done.5
  109.5 0.9 shard_map.99
  (1 shorter events, 0.0 us)
Async XLA Ops:
  0.0 1.1 %copy-start = (bf16[1024,384]{1,0:T(8,128)(2,1)S(1)}, bf16[1024,384]{1,0:T(8,128)(2,1)}, u32[]{:S(2)}) copy-start(bf16[1024,384]{1,0:T(8,128)(2,1)} %raw.5) | copy-start | bytes 2359300
  1.1 17.6 %copy-start.1 = (bf16[1024,384]{1,0:T(8,128)(2,1)S(1)}, bf16[1024,384]{1,0:T(8,128)(2,1)}, u32[]{:S(2)}) copy-start(bf16[1024,384]{1,0:T(8,128)(2,1)} %raw.5) | copy-start | bytes 2359300
  1.1 17.6 %copy-start.4 = (bf16[384,384]{1,0:T(8,128)(2,1)S(1)}, bf16[384,384]{1,0:T(8,128)(2,1)}, u32[]{:S(2)}) copy-start(bf16[384,384]{1,0:T(8,128)(2,1)} %whitening.3) | copy-start | bytes 884740
  1.2 20.9 %collective-permute-start = (bf16[128,384]{1,0:T(8,128)(2,1)S(1)}, bf16[128,384]{1,0:T(8,128)(2,1)S(1)}, u32[]{:S(2)}, u32[]{:S(2)}) collective-permute-start(bf16[128,384]{1,0:T(8,128)(2,1)S(1)} %get-tuple-element.21), channel_id=1, source_target_pairs={{0,8},{8,16},{16,24},{24,32},{32,40},{40,48},{48,56},{56,64},{64,7... | collective-permute-start | bytes 294920 | tf_op jit(solution)/shard_map/ppermute | solution.py:378
  5.1 16.9 %collective-permute-start.1 = (bf16[64,384]{1,0:T(8,128)(2,1)S(1)}, bf16[64,384]{1,0:T(8,128)(2,1)S(1)}, u32[]{:S(2)}, u32[]{:S(2)}) collective-permute-start(bf16[64,384]{1,0:T(8,128)(2,1)S(1)} %get-tuple-element.22), channel_id=1, source_target_pairs={{8,0},{16,8},{24,16},{32,24},{40,32},{48,40},{56,48},{64,56},{72,6... | collective-permute-start | bytes 147464 | tf_op jit(solution)/shard_map/ppermute | solution.py:379
  14.8 0.7 copy-start.6
  15.5 0.7 copy-start.7
  16.1 0.7 copy-start.8
  18.7 3.3 %copy-start.2 = (bf16[2304,384]{1,0:T(8,128)(2,1)S(1)}, bf16[2304,384]{1,0:T(8,128)(2,1)}, u32[]{:S(2)}) copy-start(bf16[2304,384]{1,0:T(8,128)(2,1)} %project.1) | copy-start | bytes 5308420
  22.0 15.6 %copy-start.3 = (bf16[1,1024,384]{2,1,0:T(8,128)(2,1)S(1)}, bf16[1,1024,384]{2,1,0:T(8,128)(2,1)}, u32[]{:S(2)}) copy-start(bf16[1,1024,384]{2,1,0:T(8,128)(2,1)} %centers.3) | copy-start | bytes 2359300
  49.9 59.6 %copy-start.5 = (f32[1,64]{1,0:T(1,128)S(1)}, f32[1,64]{1,0:T(1,128)}, u32[]{:S(2)}) copy-start(f32[1,64]{1,0:T(1,128)} %prior.1) | copy-start | bytes 772
  73.1 19.1 %collective-permute-start.2 = (bf16[208,128]{1,0:T(8,128)(2,1)S(1)}, bf16[208,128]{1,0:T(8,128)(2,1)S(1)}, u32[]{:S(2)}, u32[]{:S(2)}) collective-permute-start(bf16[208,128]{1,0:T(8,128)(2,1)S(1)} %get-tuple-element.32), channel_id=1, source_target_pairs={{0,32},{8,40},{16,48},{24,56},{32,64},{40,72},{48,80},{56,88},{64,... | collective-permute-start | bytes 159752 | tf_op jit(solution)/shard_map/ppermute | solution.py:394
  78.7 15.4 %collective-permute-start.3 = (bf16[208,128]{1,0:T(8,128)(2,1)S(1)}, bf16[208,128]{1,0:T(8,128)(2,1)S(1)}, u32[]{:S(2)}, u32[]{:S(2)}) collective-permute-start(bf16[208,128]{1,0:T(8,128)(2,1)S(1)} %get-tuple-element.33), channel_id=1, source_target_pairs={{0,64},{8,72},{16,80},{24,88},{32,96},{40,104},{48,112},{56,120},{... | collective-permute-start | bytes 159752 | tf_op jit(solution)/shard_map/ppermute | solution.py:394
  86.7 10.8 %collective-permute-start.4 = (bf16[208,128]{1,0:T(8,128)(2,1)S(1)}, bf16[208,128]{1,0:T(8,128)(2,1)S(1)}, u32[]{:S(2)}, u32[]{:S(2)}) collective-permute-start(bf16[208,128]{1,0:T(8,128)(2,1)S(1)} %get-tuple-element.34), channel_id=1, source_target_pairs={{0,96},{8,104},{16,112},{24,120},{32,0},{40,8},{48,16},{56,24},{64... | collective-permute-start | bytes 159752 | tf_op jit(solution)/shard_map/ppermute | solution.py:394
  97.6 6.0 %collective-permute-start.5 = (bf16[208,128]{1,0:T(8,128)(2,1)S(1)}, bf16[208,128]{1,0:T(8,128)(2,1)S(1)}, u32[]{:S(2)}, u32[]{:S(2)}) collective-permute-start(bf16[208,128]{1,0:T(8,128)(2,1)S(1)} %get-tuple-element.36), channel_id=1, source_target_pairs={{0,128},{128,256},{256,384},{1,129},{129,257},{257,385},{2,130},{1... | collective-permute-start | bytes 159752 | tf_op jit(solution)/shard_map/ppermute | solution.py:399
  98.9 7.6 %collective-permute-start.6 = (bf16[208,128]{1,0:T(8,128)(2,1)S(1)}, bf16[208,128]{1,0:T(8,128)(2,1)S(1)}, u32[]{:S(2)}, u32[]{:S(2)}) collective-permute-start(bf16[208,128]{1,0:T(8,128)(2,1)S(1)} %get-tuple-element.36), channel_id=1, source_target_pairs={{0,256},{128,384},{1,257},{129,385},{2,258},{130,386},{3,259},{131... | collective-permute-start | bytes 159752 | tf_op jit(solution)/shard_map/ppermute | solution.py:399
  100.2 9.3 %collective-permute-start.7 = (bf16[208,128]{1,0:T(8,128)(2,1)S(1)}, bf16[208,128]{1,0:T(8,128)(2,1)S(1)}, u32[]{:S(2)}, u32[]{:S(2)}) collective-permute-start(bf16[208,128]{1,0:T(8,128)(2,1)S(1)} %get-tuple-element.36), channel_id=1, source_target_pairs={{0,384},{1,385},{2,386},{3,387},{4,388},{5,389},{6,390},{7,391},{8... | collective-permute-start | bytes 159752 | tf_op jit(solution)/shard_map/ppermute | solution.py:399

commit v6 on v5

--- a/solution.py
+++ b/solution.py
@@ -303,34 +303,30 @@
     )(shares, weights, tops, spikes)
 
 
-def near_kernel(got, own, one, two, three):
+def near_kernel(got, out):
     front = lax.broadcasted_iota(jnp.int32, (1, 128), 1) < ROWS
     slot = lax.broadcasted_iota(jnp.int32, (16, 128), 0)
-    mine = lax.axis_index("lane") // NEAR
     tails = got[0, FAR * SUM_ROWS : NEAR_ROWS, :].astype(F32)
     for n in range(1, NEAR):
         tails = tails + got[n, FAR * SUM_ROWS : NEAR_ROWS, :].astype(F32)
-    for d, out in enumerate((own, one, two, three)):
-        far = lax.rem(mine + d, FAR)
-        part = pl.ds(pl.multiple_of(far * SUM_ROWS, 64), SUM_ROWS)
+    for far in range(FAR):
+        part = slice(far * SUM_ROWS, (far + 1) * SUM_ROWS)
         acc = got[0, part, :].astype(F32)
         for n in range(1, NEAR):
             acc = acc + got[n, part, :].astype(F32)
         tail = jnp.sum(jnp.where(slot == far, tails, 0.0), axis=0, keepdims=True)
-        mass = tail + pltpu.roll(tail, ROWS, 1)
-        out[0:SUM_ROWS, :] = acc.astype(out.dtype)
-        if d == 0:
-            out[SUM_ROWS:PAY, :] = jnp.broadcast_to(mass, (PAY - SUM_ROWS, 128))
-        else:
-            out[SUM_ROWS:PAY, :] = split(mass, front)
-
-
-def far_kernel(own, one, two, three, out, sent):
+        out[far, 0:SUM_ROWS, :] = acc.astype(BF16)
+        out[far, SUM_ROWS:PAY, :] = split(tail + pltpu.roll(tail, ROWS, 1), front)
+
+
+def far_kernel(got, out, sent):
     front = lax.broadcasted_iota(jnp.int32, (1, 128), 1) < ROWS
-    acc = one[...].astype(F32) + two[...].astype(F32) + three[...].astype(F32)
-    total = own[0:SUM_ROWS, :] + acc[0:SUM_ROWS]
+    acc = got[0].astype(F32)
+    for f in range(1, FAR):
+        acc = acc + got[f].astype(F32)
+    total = acc[0:SUM_ROWS]
     tail = acc[SUM_ROWS:PAY, :]
-    mass = own[SUM_ROWS:PAY, :] + tail + pltpu.roll(tail, ROWS, 1)
+    mass = tail + pltpu.roll(tail, ROWS, 1)
     out[0:SUM_ROWS, :] = total
     out[SUM_ROWS:PAY, :] = mass
     sent[0:SUM_ROWS, :] = total.astype(BF16)
@@ -387,14 +383,11 @@
     got = lax.all_to_all(parts, "lane", 0, 0, axis_index_groups=near)
     small = jax.ShapeDtypeStruct((PAY, 128), BF16)
     wide = jax.ShapeDtypeStruct((PAY, 128), F32)
-    own, *sent = call(
-        near_kernel, (wide, small, small, small), [VMEM], (VMEM,) * 4, moved=1_000_000
-    )(got)
-    took = [
-        lax.ppermute(part, "lane", [(i, (i + NEAR * (d + 1)) % LANES) for i in range(LANES)])
-        for d, part in enumerate(sent)
-    ]
-    total, sent = call(far_kernel, (wide, small), [VMEM] * 4, (VMEM,) * 2, moved=300_000)(own, *took)
+    far = [[NEAR * f + n for f in range(FAR)] for n in range(NEAR)]
+    block = jax.ShapeDtypeStruct((FAR, PAY, 128), BF16)
+    halves = call(near_kernel, block, [VMEM], VMEM, moved=1_000_000)(got)
+    halves = lax.all_to_all(halves, "lane", 0, 0, axis_index_groups=far)
+    total, sent = call(far_kernel, (wide, small), [VMEM], (VMEM,) * 2, moved=300_000)(halves)
     earlier = [
         lax.ppermute(sent, "section", [(i, i + d) for i in range(SECTIONS - d)])
         for d in range(1, SECTIONS)

time: 111 us -> 112 us (level)
  the two profiles are of different devices: /device:TPU:24 before, /device:TPU:56 now
where the time goes in v6:
time: 112 us
  blocking collectives  79.5 us (71%)
  Pallas kernels  10.7 us (10%)
  starting transfers between devices  9.84 us (9%)
  waiting for transfers between devices  8.02 us (7%)
  local copies, waits for them, and re-layouts  3.15 us (3%)
    all_to_all x1, blocking collectives, per_device(): got = lax.all_to_all(parts, 'lane', 0, 0, axis_index_groups=near)  29.3 us
    all_to_all x1, blocking collectives, per_device(): halves = lax.all_to_all(halves, 'lane', 0, 0, axis_index_groups=far)  27.5 us
    all_gather x1, blocking collectives, per_device(): spikes = lax.all_gather(feats, 'group', axis=0, tiled=True)  13.7 us
    all_to_all x1, blocking collectives, per_device(): shares = lax.all_to_all(shares, 'group', 0, 0)  9.05 us
    ppermute x3, waiting for transfers between devices, per_device(): lax.ppermute(sent, 'section', [(i, i + d) for i in range(SECTIONS - d)])  8.02 us
    ppermute x1, starting transfers between devices, per_device(): before = lax.ppermute(tail, windows, [(i, i + 1) for i in range(count - 1)])  3.96 us
    ppermute x3, starting transfers between devices, per_device(): lax.ppermute(sent, 'section', [(i, i + d) for i in range(SECTIONS - d)])  3.86 us
    unnamed x18, local copies, waits for them, and re-layouts  3.15 us
  transfers between devices with their start and end apart: 5, of which 3 were waited for; matrix products, arithmetic and copies ran while one was open for 0% of the time, Pallas kernels for 4%

profile of v6, /device:TPU:56, one launch (start us, length us, event | category | flops | bytes accessed | tf_op | source)
XLA Modules:
  0.0 112.0 jit_solution(10697939964408449992)
XLA Ops:
  0.0 0.0 copy-start
  0.0 1.1 %copy-done = bf16[1024,384]{1,0:T(8,128)(2,1)S(1)} copy-done((bf16[1024,384]{1,0:T(8,128)(2,1)S(1)}, bf16[1024,384]{1,0:T(8,128)(2,1)}, u32[]{:S(2)}) %copy-start) | copy-done | bytes 786456
  1.1 0.0 copy-start.1
  1.1 0.0 copy-start.4
  1.2 4.0 %collective-permute-start = (bf16[128,384]{1,0:T(8,128)(2,1)S(1)}, bf16[128,384]{1,0:T(8,128)(2,1)S(1)}, u32[]{:S(2)}, u32[]{:S(2)}) collective-permute-start(bf16[128,384]{1,0:T(8,128)(2,1)S(1)} %get-tuple-element.17), channel_id=1, source_target_pairs={{0,8},{8,16},{16,24},{24,32},{32,40},{40,48},{48,56},{56,64},{64,7... | collective-permute-start | bytes 294920 | tf_op jit(solution)/shard_map/ppermute | solution.py:374
  5.1 2.0 %collective-permute-start.1 = (bf16[64,384]{1,0:T(8,128)(2,1)S(1)}, bf16[64,384]{1,0:T(8,128)(2,1)S(1)}, u32[]{:S(2)}, u32[]{:S(2)}) collective-permute-start(bf16[64,384]{1,0:T(8,128)(2,1)S(1)} %get-tuple-element.18), channel_id=1, source_target_pairs={{8,0},{16,8},{24,16},{32,24},{40,32},{48,40},{56,48},{64,56},{72,6... | collective-permute-start | bytes 147464 | tf_op jit(solution)/shard_map/ppermute | solution.py:375
  7.1 0.0 copy-start.6
  7.2 0.7 copy-done.6
  7.8 0.0 copy-start.7
  7.8 0.7 copy-done.7
  8.5 0.0 copy-start.8
  8.5 0.7 copy-done.8
  9.1 1.9 %shard_map.92 = (bf16[1024,896]{1,0:T(8,128)(2,1)S(1)}, bf16[1024,384]{1,0:T(8,128)(2,1)S(1)}, bf16[384,256]{1,0:T(8,128)(2,1)S(1)}) custom-call(f32[1,64]{1,0:T(1,128)S(1)} %bitcast.3, bf16[6,121]{1,0:T(8,128)(2,1)S(1)} %bitcast.2, s32[1,1,128]{2,1,0:T(1,128)S(1)} %copy-done.8), custom_call_target="tpu_custom_call" | custom-call | flops 500000000 | bytes 8000000 | tf_op jit(solution)/shard_map/pallas_call | solution.py:114
  11.0 0.0 copy-done.1
  11.0 0.0 copy-done.4
  11.0 0.0 copy-start.2
  11.1 2.6 %shard_map.93 = (f32[1024,384]{1,0:T(8,128)S(1)}, bf16[960,384]{1,0:T(8,128)(2,1)S(1)}) custom-call(bf16[1024,384]{1,0:T(8,128)(2,1)S(1)} %copy-done.1, bf16[384,384]{1,0:T(8,128)(2,1)S(1)} %copy-done.4, bf16[1024,896]{1,0:T(8,128)(2,1)S(1)} %get-tuple-element.19.core, bf16[384,256]{1,0:T(8,128)(2,1)S(1)} %get-tuple-element.20.band), custom_call_target="tpu_custom_call" | custom-call | flops 2000000000 | bytes 6000000 | tf_op jit(solution)/shard_map/pallas_call | solution.py:131
  14.3 0.0 collective-permute-done.1.after
  14.3 0.0 collective-permute-done.before
  14.4 0.0 copy-done.2
  14.4 0.0 copy-start.3
  14.4 1.9 %shard_map.94 = bf16[128,384]{1,0:T(8,128)(2,1)S(1)} custom-call(bf16[128,384]{1,0:T(8,128)(2,1)S(1)} %collective-permute-done.before, bf16[64,384]{1,0:T(8,128)(2,1)S(1)} %collective-permute-done.1.after, bf16[1024,384]{1,0:T(8,128)(2,1)S(1)} %copy-done.1, bf16[384,384]{1,0:T(8,128)(2,1)S(1)} %copy-done.4, f32[1024,384]{1,0:T(8,128)S(1)} %get-tuple-element.21.found, ...), custom_call_target="tpu_custom_call" | custom-call | flops 1000000000 | bytes 6000000 | tf_op jit(solution)/shard_map/pallas_call | solution.py:183
  16.3 13.7 %all_gather.3.spikes = bf16[1024,384]{1,0:T(8,128)(2,1)S(1)} all-gather(bf16[128,384]{1,0:T(8,128)(2,1)S(1)} %shard_map.94), channel_id=1, replica_groups=mesh['section'=4,'lane'=16,'group'=8] {'group'}, dimensions={0}, use_global_device_ids=true | all-gather | bytes 884736 | tf_op jit(solution)/shard_map/all_gather | solution.py:378
  30.0 0.0 copy-done.3
  30.0 2.0 %shard_map.95 = (f32[8,8,128]{2,1,0:T(8,128)S(1)}, bf16[1024,1024]{1,0:T(8,128)(2,1)S(1)}, f32[8,128]{1,0:T(8,128)S(1)}) custom-call(bf16[1024,384]{1,0:T(8,128)(2,1)S(1)} %all_gather.3.spikes, bf16[1,1024,384]{2,1,0:T(8,128)(2,1)S(1)} %copy-done.3, s32[1,1]{1,0:T(1,128)S(6)} %copy.10.counts), custom_call_target="tpu_custom_call" | custom-call | flops 1000000000 | bytes 4000000 | tf_op jit(solution)/shard_map/pallas_call | solution.py:229
  32.0 9.0 %all_to_all.15.shares = f32[8,8,128]{2,1,0:T(8,128)S(1)} all-to-all(f32[8,8,128]{2,1,0:T(8,128)S(1)} %get-tuple-element.24), channel_id=1, replica_groups=mesh['section'=4,'lane'=16,'group'=8] {'group'}, dimensions={0} | all-to-all | bytes 65536 | tf_op jit(solution)/shard_map/all_to_all | solution.py:380
  41.0 1.3 %shard_map.96 = bf16[4,784,128]{2,1,0:T(8,128)(2,1)S(1)} custom-call(f32[8,8,128]{2,1,0:T(8,128)S(1)} %all_to_all.15.shares, bf16[1024,1024]{1,0:T(8,128)(2,1)S(1)} %get-tuple-element.25.weights, f32[8,128]{1,0:T(8,128)S(1)} %get-tuple-element.26.tops, bf16[1024,384]{1,0:T(8,128)(2,1)S(1)} %all_gather.3.spikes), custom_call_target="tpu_custom_call" | custom-call | flops 1000000000 | bytes 4000000 | tf_op jit(solution)/shard_map/pallas_call | solution.py:296
  42.3 0.0 copy-start.5
  42.3 29.3 %all_to_all.16.got = bf16[4,784,128]{2,1,0:T(8,128)(2,1)S(1)} all-to-all(bf16[4,784,128]{2,1,0:T(8,128)(2,1)S(1)} %shard_map.96), channel_id=1, replica_groups={{0,8,16,24},{32,40,48,56},{64,72,80,88},{96,104,112,120},{1,9,17,25},{3..., dimensions={0} | all-to-all | bytes 1605632 | tf_op jit(solution)/shard_map/all_to_all | solution.py:383
  71.6 0.1 shard_map.97
  71.7 27.5 %all_to_all.17.got = bf16[4,208,128]{2,1,0:T(8,128)(2,1)S(1)} all-to-all(bf16[4,208,128]{2,1,0:T(8,128)(2,1)S(1)} %shard_map.97), channel_id=1, replica_groups={{0,32,64,96},{8,40,72,104},{16,48,80,112},{24,56,88,120},{1,33,65,97},{..., dimensions={0} | all-to-all | bytes 425984 | tf_op jit(solution)/shard_map/all_to_all | solution.py:389
  99.2 0.1 shard_map.98
  99.3 1.3 %collective-permute-start.2 = (bf16[208,128]{1,0:T(8,128)(2,1)S(1)}, bf16[208,128]{1,0:T(8,128)(2,1)S(1)}, u32[]{:S(2)}, u32[]{:S(2)}) collective-permute-start(bf16[208,128]{1,0:T(8,128)(2,1)S(1)} %get-tuple-element.28), channel_id=1, source_target_pairs={{0,128},{128,256},{256,384},{1,129},{129,257},{257,385},{2,130},{1... | collective-permute-start | bytes 159752 | tf_op jit(solution)/shard_map/ppermute | solution.py:392
  100.5 1.3 %collective-permute-start.3 = (bf16[208,128]{1,0:T(8,128)(2,1)S(1)}, bf16[208,128]{1,0:T(8,128)(2,1)S(1)}, u32[]{:S(2)}, u32[]{:S(2)}) collective-permute-start(bf16[208,128]{1,0:T(8,128)(2,1)S(1)} %get-tuple-element.28), channel_id=1, source_target_pairs={{0,256},{128,384},{1,257},{129,385},{2,258},{130,386},{3,259},{131... | collective-permute-start | bytes 159752 | tf_op jit(solution)/shard_map/ppermute | solution.py:392
  101.8 1.3 %collective-permute-start.4 = (bf16[208,128]{1,0:T(8,128)(2,1)S(1)}, bf16[208,128]{1,0:T(8,128)(2,1)S(1)}, u32[]{:S(2)}, u32[]{:S(2)}) collective-permute-start(bf16[208,128]{1,0:T(8,128)(2,1)S(1)} %get-tuple-element.28), channel_id=1, source_target_pairs={{0,384},{1,385},{2,386},{3,387},{4,388},{5,389},{6,390},{7,391},{8... | collective-permute-start | bytes 159752 | tf_op jit(solution)/shard_map/ppermute | solution.py:392
  103.1 2.1 %collective-permute-done.2.one = bf16[208,128]{1,0:T(8,128)(2,1)S(1)} collective-permute-done((bf16[208,128]{1,0:T(8,128)(2,1)S(1)}, bf16[208,128]{1,0:T(8,128)(2,1)S(1)}, u32[]{:S(2)}, u32[]{:S(2)}) %collective-permute-start.2) | collective-permute-done | bytes 53280 | tf_op jit(solution)/shard_map/ppermute | solution.py:392
  105.3 2.8 %collective-permute-done.3.two = bf16[208,128]{1,0:T(8,128)(2,1)S(1)} collective-permute-done((bf16[208,128]{1,0:T(8,128)(2,1)S(1)}, bf16[208,128]{1,0:T(8,128)(2,1)S(1)}, u32[]{:S(2)}, u32[]{:S(2)}) %collective-permute-start.3) | collective-permute-done | bytes 53280 | tf_op jit(solution)/shard_map/ppermute | solution.py:392
  108.1 3.1 %collective-permute-done.4.three = bf16[208,128]{1,0:T(8,128)(2,1)S(1)} collective-permute-done((bf16[208,128]{1,0:T(8,128)(2,1)S(1)}, bf16[208,128]{1,0:T(8,128)(2,1)S(1)}, u32[]{:S(2)}, u32[]{:S(2)}) %collective-permute-start.4) | collective-permute-done | bytes 53280 | tf_op jit(solution)/shard_map/ppermute | solution.py:392
  111.2 0.0 copy-done.5
  111.2 0.9 shard_map.99
  (1 shorter events, 0.0 us)
Async XLA Ops:
  0.0 1.1 %copy-start = (bf16[1024,384]{1,0:T(8,128)(2,1)S(1)}, bf16[1024,384]{1,0:T(8,128)(2,1)}, u32[]{:S(2)}) copy-start(bf16[1024,384]{1,0:T(8,128)(2,1)} %raw.5) | copy-start | bytes 2359300
  1.1 9.9 %copy-start.1 = (bf16[1024,384]{1,0:T(8,128)(2,1)S(1)}, bf16[1024,384]{1,0:T(8,128)(2,1)}, u32[]{:S(2)}) copy-start(bf16[1024,384]{1,0:T(8,128)(2,1)} %raw.5) | copy-start | bytes 2359300
  1.1 9.9 %copy-start.4 = (bf16[384,384]{1,0:T(8,128)(2,1)S(1)}, bf16[384,384]{1,0:T(8,128)(2,1)}, u32[]{:S(2)}) copy-start(bf16[384,384]{1,0:T(8,128)(2,1)} %whitening.3) | copy-start | bytes 884740
  1.2 13.2 %collective-permute-start = (bf16[128,384]{1,0:T(8,128)(2,1)S(1)}, bf16[128,384]{1,0:T(8,128)(2,1)S(1)}, u32[]{:S(2)}, u32[]{:S(2)}) collective-permute-start(bf16[128,384]{1,0:T(8,128)(2,1)S(1)} %get-tuple-element.17), channel_id=1, source_target_pairs={{0,8},{8,16},{16,24},{24,32},{32,40},{40,48},{48,56},{56,64},{64,7... | collective-permute-start | bytes 294920 | tf_op jit(solution)/shard_map/ppermute | solution.py:374
  5.1 9.2 %collective-permute-start.1 = (bf16[64,384]{1,0:T(8,128)(2,1)S(1)}, bf16[64,384]{1,0:T(8,128)(2,1)S(1)}, u32[]{:S(2)}, u32[]{:S(2)}) collective-permute-start(bf16[64,384]{1,0:T(8,128)(2,1)S(1)} %get-tuple-element.18), channel_id=1, source_target_pairs={{8,0},{16,8},{24,16},{32,24},{40,32},{48,40},{56,48},{64,56},{72,6... | collective-permute-start | bytes 147464 | tf_op jit(solution)/shard_map/ppermute | solution.py:375
  7.1 0.7 copy-start.6
  7.8 0.7 copy-start.7
  8.5 0.7 copy-start.8
  11.0 3.3 %copy-start.2 = (bf16[2304,384]{1,0:T(8,128)(2,1)S(1)}, bf16[2304,384]{1,0:T(8,128)(2,1)}, u32[]{:S(2)}) copy-start(bf16[2304,384]{1,0:T(8,128)(2,1)} %project.1) | copy-start | bytes 5308420
  14.4 15.6 %copy-start.3 = (bf16[1,1024,384]{2,1,0:T(8,128)(2,1)S(1)}, bf16[1,1024,384]{2,1,0:T(8,128)(2,1)}, u32[]{:S(2)}) copy-start(bf16[1,1024,384]{2,1,0:T(8,128)(2,1)} %centers.3) | copy-start | bytes 2359300
  42.3 68.9 %copy-start.5 = (f32[1,64]{1,0:T(1,128)S(1)}, f32[1,64]{1,0:T(1,128)}, u32[]{:S(2)}) copy-start(f32[1,64]{1,0:T(1,128)} %prior.1) | copy-start | bytes 772
  99.3 6.0 %collective-permute-start.2 = (bf16[208,128]{1,0:T(8,128)(2,1)S(1)}, bf16[208,128]{1,0:T(8,128)(2,1)S(1)}, u32[]{:S(2)}, u32[]{:S(2)}) collective-permute-start(bf16[208,128]{1,0:T(8,128)(2,1)S(1)} %get-tuple-element.28), channel_id=1, source_target_pairs={{0,128},{128,256},{256,384},{1,129},{129,257},{257,385},{2,130},{1... | collective-permute-start | bytes 159752 | tf_op jit(solution)/shard_map/ppermute | solution.py:392
  100.5 7.5 %collective-permute-start.3 = (bf16[208,128]{1,0:T(8,128)(2,1)S(1)}, bf16[208,128]{1,0:T(8,128)(2,1)S(1)}, u32[]{:S(2)}, u32[]{:S(2)}) collective-permute-start(bf16[208,128]{1,0:T(8,128)(2,1)S(1)} %get-tuple-element.28), channel_id=1, source_target_pairs={{0,256},{128,384},{1,257},{129,385},{2,258},{130,386},{3,259},{131... | collective-permute-start | bytes 159752 | tf_op jit(solution)/shard_map/ppermute | solution.py:392
  101.8 9.3 %collective-permute-start.4 = (bf16[208,128]{1,0:T(8,128)(2,1)S(1)}, bf16[208,128]{1,0:T(8,128)(2,1)S(1)}, u32[]{:S(2)}, u32[]{:S(2)}) collective-permute-start(bf16[208,128]{1,0:T(8,128)(2,1)S(1)} %get-tuple-element.28), channel_id=1, source_target_pairs={{0,384},{1,385},{2,386},{3,387},{4,388},{5,389},{6,390},{7,391},{8... | collective-permute-start | bytes 159752 | tf_op jit(solution)/shard_map/ppermute | solution.py:392
